TPU v7x, 512 devices: a whole 4x4x16 slice. The times are simulated.
512 devices in a mesh: cfg: 2 (over y_lo), seq: 32 (over z, core), head: 8 (over y_hi, x).
Axes of the slice: x: 4, y: 4 (y_hi: 2, y_lo: 2; y = y_hi * 2 + y_lo), z: 16, core: 2. Of those that a mesh axis runs over, the one named last changes fastest.
Arguments:
- queries: bfloat16 [49152, 5120], P(('cfg', 'seq', 'head')), parts along dimension 0, may hold values from -90 to 90
- keys: bfloat16 [49152, 5120], P(('cfg', 'seq', 'head')), parts along dimension 0, may hold values from -4 to 4
- values: bfloat16 [49152, 5120], P(('cfg', 'seq', 'head')), parts along dimension 0, may hold values from -6 to 6
- windows: int32 [40, 3], replicated, may hold values from 0 to 1, as said below
Outputs:
- attended: bfloat16 [49152, 5120], P(('cfg', 'seq', 'head')), parts along dimension 0
There are 2 independent parts, one for each index of `cfg`. A program takes and returns all parts, laid end to end along the dimension named above; an argument that names none is the same for every part. Nothing has to cross between parts.
Inputs may be any that keep to these rules, and one draw needn't show every extreme that they name: `windows`: each extent is 0 or 1; some head has all three extents 1 and another all three 0.
All inputs are finite; a program needn't handle non-finite values.
Results may differ from a plain program's by a relative error of at most 0.0046.
Values may be sent and summed in bfloat16 or wider, within the bound.
No kernel may reach another device: no remote copies, remote signals or barrier semaphores. Data moves between devices by JAX's collectives and lax.ppermute only.
A program may use at most 128 MiB of HBM per device.

v0:
```python
import jax
import jax.numpy as jnp
from jax import lax
from jax.sharding import PartitionSpec as P

HD = 128
TILE = 384
TW = 1


def padded(cells, sides, width):
    for axis, dim in sides:
        count = lax.axis_size(axis)
        ends = count - 1
        head = lax.slice_in_dim(cells, 0, width, axis=dim)
        tail = lax.slice_in_dim(cells, cells.shape[dim] - width, cells.shape[dim], axis=dim)
        cells = jnp.concatenate(
            [
                lax.ppermute(tail, axis, [(i, (i + 1) % count) for i in range(ends)]),
                cells,
                lax.ppermute(head, axis, [((i + 1) % count, i) for i in range(ends)]),
            ],
            axis=dim,
        )
    return cells


def finish(scores, value_h, extent, lay_gap, row_gap, col_gap, inside):
    visible = (
        (lay_gap[None, :] <= extent[0])
        & (row_gap <= extent[1])
        & (col_gap <= extent[2])
        & inside[None, :]
    )
    scores = jnp.where(visible, scores, -jnp.inf)
    largest = jnp.max(scores, axis=-1, keepdims=True)
    weights = jnp.exp(scores - largest)
    total = jnp.sum(weights, axis=-1, keepdims=True)
    probs = weights.astype(jnp.bfloat16)
    mixed = jnp.dot(probs, value_h, preferred_element_type=jnp.float32) / total
    return mixed.astype(jnp.bfloat16)


def layer_rim_pairs(paired, lrows, local_heads, width):
    extended = padded(paired, (("seq", 0),), lrows)
    key_heads = jnp.transpose(extended[:, :width].reshape(3 * lrows, local_heads, HD), (1, 0, 2))
    value_heads = jnp.transpose(extended[:, width:].reshape(3 * lrows, local_heads, HD), (1, 0, 2))
    return (key_heads, value_heads)


def shards(queries, keys, values, windows):
    slab_q, slab_k, slab_v = (
        lax.all_to_all(queries, "head", split_axis=1, concat_axis=0, tiled=True),
        lax.all_to_all(keys, "head", split_axis=1, concat_axis=0, tiled=True),
        lax.all_to_all(values, "head", split_axis=1, concat_axis=0, tiled=True),
    )
    lrows = slab_q.shape[0]
    local_heads = slab_q.shape[1] // HD
    width = local_heads * HD
    scale = HD ** (-0.5)
    head_win = lax.dynamic_slice_in_dim(
        windows, lax.axis_index("head") * local_heads, local_heads, 0
    )
    nlayers = lax.axis_size("seq")
    layer_index = lax.axis_index("seq")
    q_tile = jnp.arange(lrows, dtype=jnp.int32) // TILE
    k_index = jnp.arange(3 * lrows, dtype=jnp.int32)
    k_tile = k_index % lrows // TILE
    k_layer = k_index // lrows - 1
    row_gap = jnp.abs(q_tile[:, None] // TW - k_tile[None, :] // TW)
    col_gap = jnp.abs(q_tile[:, None] % TW - k_tile[None, :] % TW)
    lay_gap = jnp.abs(k_layer)
    inside = (layer_index + k_layer >= 0) & (layer_index + k_layer < nlayers)
    query_heads = jnp.transpose(slab_q.reshape(lrows, local_heads, HD), (1, 0, 2))
    paired = jnp.concatenate([slab_k, slab_v], axis=1)
    key_heads, value_heads = layer_rim_pairs(paired, lrows, local_heads, width)

    def one_head(items):
        query_h, key_h, value_h, extent = items
        scores = (
            lax.dot_general(
                query_h, key_h, (((1,), (1,)), ((), ())), preferred_element_type=jnp.float32
            )
            * scale
        )
        return finish(scores, value_h, extent, lay_gap, row_gap, col_gap, inside)

    outputs = lax.map(one_head, (query_heads, key_heads, value_heads, head_win))
    result = jnp.transpose(outputs, (1, 0, 2)).reshape(lrows, width)
    return lax.all_to_all(result, "head", split_axis=0, concat_axis=1, tiled=True)


def solution(mesh):
    placed = (
        P(("cfg", "seq", "head"), None),
        P(("cfg", "seq", "head"), None),
        P(("cfg", "seq", "head"), None),
        P(),
    )
    return jax.shard_map(
        shards,
        mesh=mesh,
        in_specs=placed,
        out_specs=P(("cfg", "seq", "head"), None),
        check_vma=False,
    )
```

profile of v0, /device:TPU:1, one launch (start us, length us, event | category | flops | bytes accessed | tf_op | source)
XLA Modules:
  0.0 182.4 jit_solution(12443316195280415686)
XLA Ops:
  0.0 2.2 %copy.58 = bf16[12,8,8,640]{3,2,0,1:T(8,128)(2,1)} copy(bf16[12,8,8,640]{3,2,1,0:T(8,128)(2,1)} %bitcast.79) | data formatting | bytes 1966080 | tf_op jit(solution)/shard_map/all_to_all | solution.py:54
  2.2 7.5 %all-to-all-start.1 = ((bf16[96,8,640]{2,0,1:T(8,128)(2,1)}), bf16[96,8,640]{2,0,1:T(8,128)(2,1)S(1)}, u32[]{:S(2)}, u32[]{:S(2)}) async-start(bf16[96,8,640]{2,0,1:T(8,128)(2,1)} %bitcast.53), calls=%async_computation.1 | async-start | bytes 1966080 | tf_op jit(solution)/shard_map/all_to_all | solution.py:54
  9.7 1.3 copy.57
  11.0 15.0 %all-to-all-done.1 = bf16[96,8,640]{2,0,1:T(8,128)(2,1)S(1)} async-done(((bf16[96,8,640]{2,0,1:T(8,128)(2,1)}), bf16[96,8,640]{2,0,1:T(8,128)(2,1)S(1)}, u32[]{:S(2)}, u32[]{:S(2)}) %all-to-all-start.1) | async-done | bytes 983072 | tf_op jit(solution)/shard_map/all_to_all | solution.py:54
  26.0 17.7 %all_to_all.73 = bf16[96,8,640]{2,0,1:T(8,128)(2,1)S(1)} all-to-all(bf16[96,8,640]{2,0,1:T(8,128)(2,1)S(1)} %bitcast.76), channel_id=1, replica_groups=mesh['cfg'=2,'seq'=32,'head'=8] {'head'}, dimensions={1} | all-to-all | bytes 1966080 | tf_op jit(solution)/shard_map/all_to_all | solution.py:55
  43.7 1.5 pad_maximum_fusion.1
  45.1 6.0 %collective-permute-start = (bf16[768,1280]{1,0:T(8,128)(2,1)}, bf16[768,1280]{1,0:T(8,128)(2,1)}, u32[]{:S(2)}, u32[]{:S(2)}) collective-permute-start(bf16[768,1280]{1,0:T(8,128)(2,1)} %pad_maximum_fusion.1), channel_id=1, source_target_pairs={{0,8},{8,16},{16,24},{24,32},{32,40},{40,48},{48,56},{56,64},{64,7... | collective-permute-start | bytes 5898248 | tf_op jit(solution)/shard_map/ppermute | solution.py:19
  51.1 1.9 %collective-permute-start.1 = (bf16[768,1280]{1,0:T(8,128)(2,1)}, bf16[768,1280]{1,0:T(8,128)(2,1)}, u32[]{:S(2)}, u32[]{:S(2)}) collective-permute-start(bf16[768,1280]{1,0:T(8,128)(2,1)} %pad_maximum_fusion.1), channel_id=1, source_target_pairs={{8,0},{16,8},{24,16},{32,24},{40,32},{48,40},{56,48},{64,56},{72,6... | collective-permute-start | bytes 5898248 | tf_op jit(solution)/shard_map/ppermute | solution.py:21
  53.0 2.3 %copy.59 = bf16[12,8,8,640]{3,2,0,1:T(8,128)(2,1)} copy(bf16[12,8,8,640]{3,2,1,0:T(8,128)(2,1)} %bitcast.81) | data formatting | bytes 1966080 | tf_op jit(solution)/shard_map/all_to_all | solution.py:53
  55.3 3.6 %all-to-all-start = ((bf16[96,8,640]{2,0,1:T(8,128)(2,1)}), bf16[96,8,640]{2,0,1:T(8,128)(2,1)S(1)}, u32[]{:S(2)}, u32[]{:S(2)}) async-start(bf16[96,8,640]{2,0,1:T(8,128)(2,1)} %bitcast.75), calls=%async_computation | async-start | bytes 1966080 | tf_op jit(solution)/shard_map/all_to_all | solution.py:53
  59.0 15.3 %all-to-all-done = bf16[96,8,640]{2,0,1:T(8,128)(2,1)S(1)} async-done(((bf16[96,8,640]{2,0,1:T(8,128)(2,1)}), bf16[96,8,640]{2,0,1:T(8,128)(2,1)S(1)}, u32[]{:S(2)}, u32[]{:S(2)}) %all-to-all-start) | async-done | bytes 983072 | tf_op jit(solution)/shard_map/all_to_all | solution.py:53
  74.2 1.0 copy-done.1
  75.2 2.3 %copy.34 = bf16[8,96,640]{1,0,2:T(8,128)(2,1)S(1)} copy(bf16[8,96,640]{2,1,0:T(8,128)(2,1)} %bitcast.74) | data formatting | bytes 1966080 | tf_op jit(solution)/shard_map/all_to_all | solution.py:53
  77.5 1.9 %reshape.113 = bf16[768,5,128]{0,2,1:T(8,128)(2,1)} reshape(bf16[8,96,640]{1,0,2:T(8,128)(2,1)S(1)} %copy.34) | data formatting | bytes 1966080 | tf_op jit(solution)/shard_map/reshape | solution.py:74
  79.4 17.2 %pad_maximum_fusion = bf16[2304,1280]{1,0:T(8,128)(2,1)} fusion(bf16[768,1280]{1,0:T(8,128)(2,1)} %collective-permute-done.1, bf16[768,640]{1,0:T(8,128)(2,1)S(1)} %bitcast.73, bf16[768,640]{1,0:T(8,128)(2,1)S(1)} %bitcast.71, bf16[768,1280]{1,0:T(8,128)(2,1)} %collective-permute-done), kind=kLoop, calls=%fused_computation.36 | loop fusion | flops 23592960 | bytes 11796480 | tf_op jit(solution)/shard_map/concatenate | solution.py:17
  96.5 4.9 %fusion.47 = (bf16[2304,640]{1,0:T(8,128)(2,1)}, bf16[2304,640]{1,0:T(8,128)(2,1)S(1)}) fusion(bf16[2304,1280]{1,0:T(8,128)(2,1)} %pad_maximum_fusion), kind=kLoop, calls=%fused_computation.60 | loop fusion | bytes 11796480 | tf_op jit(solution)/shard_map/slice | solution.py:47
  101.4 3.5 %copy.37 = bf16[2304,640]{0,1:T(8,128)(2,1)} copy(bf16[2304,640]{1,0:T(8,128)(2,1)S(1)} %get-tuple-element.172) | data formatting | bytes 5898240 | tf_op jit(solution)/shard_map/slice | solution.py:46
  104.9 3.9 %copy.38 = bf16[2304,640]{0,1:T(8,128)(2,1)S(1)} copy(bf16[2304,640]{1,0:T(8,128)(2,1)} %get-tuple-element.171) | data formatting | bytes 5898240 | tf_op jit(solution)/shard_map/slice | solution.py:47
  108.9 50.5 %while.12 = (s32[]{:T(128)}, bf16[5,768,128]{2,1,0:T(8,128)(2,1)}, s32[5,3]{0,1:T(4,128)S(1)}, bf16[5,768,128]{1,2,0:T(8,128)(2,1)}, bf16[5,2304,128]{1,2,0:T(8,...) while((s32[]{:T(128)}, bf16[5,768,128]{2,1,0:T(8,128)(2,1)}, ...), condition=%wide.region_3.4_spmd.clone, body=%wide.region_0.3_spmd.clone.sunk | while | flops 929202432 | bytes 22848688 | solution.py:88
  109.1 0.6 fusion.56
  109.7 0.7 abs_compare_fusion.3
  111.0 5.2 %fusion.57 = (f32[768]{0:T(1024)S(1)}, f32[768,2304]{1,0:T(8,128)S(1)}) fusion(bf16[5,2304,128]{1,2,0:T(8,128)(2,1)} %get-tuple-element.268, s32[]{:T(128)} %get-tuple-element.253, bf16[5,768,128]{1,2,0:T(8,128)(2,1)} %get-tuple-element.267, pred[2304]{0:T(1024)(128)(4,1)S(1)} %get-tuple-element.236, pred[]{:T(512)} %bitcast.67, s32[]{:T(128)} %bitcast.68, ...), kind=kOutput, calls=%fused_computation.59.clone.1 | convolution fusion | flops 468909312 | bytes 7886336 | tf_op jit(solution)/shard_map/while/body/eval_jaxpr/dot_general | solution.py:81
  116.2 1.1 fusion.58
  117.3 1.8 %fusion.59 = bf16[5,768,128]{2,1,0:T(8,128)(2,1)} fusion(bf16[5,768,128]{2,1,0:T(8,128)(2,1)} %get-tuple-element.254, s32[]{:T(128)} %get-tuple-element.253, f32[768,2304]{1,0:T(8,128)S(1)} %get-tuple-element.240, f32[768]{0:T(1024)S(1)} %get-tuple-element.241, bf16[5,2304,128]{1,2,0:T(8,128)(2,1)S(1)} %get-tuple-element.269, f32[768]{0:T(1024)S(1)} %fusion.58), kind=kOutput, calls=%fused_computation.16.clone.1 | convolution fusion | flops 456720384 | bytes 7873536 | tf_op jit(solution)/shard_map/while/body/eval_jaxpr/dot_general | solution.py:40
  119.2 0.6 fusion.56
  119.8 0.7 abs_compare_fusion.3
  121.1 5.2 %fusion.57 = (f32[768]{0:T(1024)S(1)}, f32[768,2304]{1,0:T(8,128)S(1)}) fusion(bf16[5,2304,128]{1,2,0:T(8,128)(2,1)} %get-tuple-element.268, s32[]{:T(128)} %get-tuple-element.253, bf16[5,768,128]{1,2,0:T(8,128)(2,1)} %get-tuple-element.267, pred[2304]{0:T(1024)(128)(4,1)S(1)} %get-tuple-element.236, pred[]{:T(512)} %bitcast.67, s32[]{:T(128)} %bitcast.68, ...), kind=kOutput, calls=%fused_computation.59.clone.1 | convolution fusion | flops 468909312 | bytes 7886336 | tf_op jit(solution)/shard_map/while/body/eval_jaxpr/dot_general | solution.py:81
  126.2 1.1 fusion.58
  127.3 1.8 %fusion.59 = bf16[5,768,128]{2,1,0:T(8,128)(2,1)} fusion(bf16[5,768,128]{2,1,0:T(8,128)(2,1)} %get-tuple-element.254, s32[]{:T(128)} %get-tuple-element.253, f32[768,2304]{1,0:T(8,128)S(1)} %get-tuple-element.240, f32[768]{0:T(1024)S(1)} %get-tuple-element.241, bf16[5,2304,128]{1,2,0:T(8,128)(2,1)S(1)} %get-tuple-element.269, f32[768]{0:T(1024)S(1)} %fusion.58), kind=kOutput, calls=%fused_computation.16.clone.1 | convolution fusion | flops 456720384 | bytes 7873536 | tf_op jit(solution)/shard_map/while/body/eval_jaxpr/dot_general | solution.py:40
  129.3 0.6 fusion.56
  129.8 0.7 abs_compare_fusion.3
  131.1 5.2 %fusion.57 = (f32[768]{0:T(1024)S(1)}, f32[768,2304]{1,0:T(8,128)S(1)}) fusion(bf16[5,2304,128]{1,2,0:T(8,128)(2,1)} %get-tuple-element.268, s32[]{:T(128)} %get-tuple-element.253, bf16[5,768,128]{1,2,0:T(8,128)(2,1)} %get-tuple-element.267, pred[2304]{0:T(1024)(128)(4,1)S(1)} %get-tuple-element.236, pred[]{:T(512)} %bitcast.67, s32[]{:T(128)} %bitcast.68, ...), kind=kOutput, calls=%fused_computation.59.clone.1 | convolution fusion | flops 468909312 | bytes 7886336 | tf_op jit(solution)/shard_map/while/body/eval_jaxpr/dot_general | solution.py:81
  136.3 1.1 fusion.58
  137.4 1.8 %fusion.59 = bf16[5,768,128]{2,1,0:T(8,128)(2,1)} fusion(bf16[5,768,128]{2,1,0:T(8,128)(2,1)} %get-tuple-element.254, s32[]{:T(128)} %get-tuple-element.253, f32[768,2304]{1,0:T(8,128)S(1)} %get-tuple-element.240, f32[768]{0:T(1024)S(1)} %get-tuple-element.241, bf16[5,2304,128]{1,2,0:T(8,128)(2,1)S(1)} %get-tuple-element.269, f32[768]{0:T(1024)S(1)} %fusion.58), kind=kOutput, calls=%fused_computation.16.clone.1 | convolution fusion | flops 456720384 | bytes 7873536 | tf_op jit(solution)/shard_map/while/body/eval_jaxpr/dot_general | solution.py:40
  139.3 0.6 fusion.56
  139.9 0.7 abs_compare_fusion.3
  141.2 5.2 %fusion.57 = (f32[768]{0:T(1024)S(1)}, f32[768,2304]{1,0:T(8,128)S(1)}) fusion(bf16[5,2304,128]{1,2,0:T(8,128)(2,1)} %get-tuple-element.268, s32[]{:T(128)} %get-tuple-element.253, bf16[5,768,128]{1,2,0:T(8,128)(2,1)} %get-tuple-element.267, pred[2304]{0:T(1024)(128)(4,1)S(1)} %get-tuple-element.236, pred[]{:T(512)} %bitcast.67, s32[]{:T(128)} %bitcast.68, ...), kind=kOutput, calls=%fused_computation.59.clone.1 | convolution fusion | flops 468909312 | bytes 7886336 | tf_op jit(solution)/shard_map/while/body/eval_jaxpr/dot_general | solution.py:81
  146.4 1.1 fusion.58
  147.4 1.8 %fusion.59 = bf16[5,768,128]{2,1,0:T(8,128)(2,1)} fusion(bf16[5,768,128]{2,1,0:T(8,128)(2,1)} %get-tuple-element.254, s32[]{:T(128)} %get-tuple-element.253, f32[768,2304]{1,0:T(8,128)S(1)} %get-tuple-element.240, f32[768]{0:T(1024)S(1)} %get-tuple-element.241, bf16[5,2304,128]{1,2,0:T(8,128)(2,1)S(1)} %get-tuple-element.269, f32[768]{0:T(1024)S(1)} %fusion.58), kind=kOutput, calls=%fused_computation.16.clone.1 | convolution fusion | flops 456720384 | bytes 7873536 | tf_op jit(solution)/shard_map/while/body/eval_jaxpr/dot_general | solution.py:40
  149.4 0.6 fusion.56
  150.0 0.7 abs_compare_fusion.3
  151.2 5.2 %fusion.57 = (f32[768]{0:T(1024)S(1)}, f32[768,2304]{1,0:T(8,128)S(1)}) fusion(bf16[5,2304,128]{1,2,0:T(8,128)(2,1)} %get-tuple-element.268, s32[]{:T(128)} %get-tuple-element.253, bf16[5,768,128]{1,2,0:T(8,128)(2,1)} %get-tuple-element.267, pred[2304]{0:T(1024)(128)(4,1)S(1)} %get-tuple-element.236, pred[]{:T(512)} %bitcast.67, s32[]{:T(128)} %bitcast.68, ...), kind=kOutput, calls=%fused_computation.59.clone.1 | convolution fusion | flops 468909312 | bytes 7886336 | tf_op jit(solution)/shard_map/while/body/eval_jaxpr/dot_general | solution.py:81
  156.4 1.1 fusion.58
  157.5 1.8 %fusion.59 = bf16[5,768,128]{2,1,0:T(8,128)(2,1)} fusion(bf16[5,768,128]{2,1,0:T(8,128)(2,1)} %get-tuple-element.254, s32[]{:T(128)} %get-tuple-element.253, f32[768,2304]{1,0:T(8,128)S(1)} %get-tuple-element.240, f32[768]{0:T(1024)S(1)} %get-tuple-element.241, bf16[5,2304,128]{1,2,0:T(8,128)(2,1)S(1)} %get-tuple-element.269, f32[768]{0:T(1024)S(1)} %fusion.58), kind=kOutput, calls=%fused_computation.16.clone.1 | convolution fusion | flops 456720384 | bytes 7873536 | tf_op jit(solution)/shard_map/while/body/eval_jaxpr/dot_general | solution.py:40
  159.3 1.9 %copy.45 = bf16[768,5,128]{2,1,0:T(8,128)(2,1)S(1)} copy(bf16[768,5,128]{2,0,1:T(8,128)(2,1)} %bitcast.10) | data formatting | bytes 1966080 | tf_op jit(solution)/shard_map/all_to_all | solution.py:90
  161.3 1.2 reshape.116
  162.5 18.9 %all_to_all.74 = bf16[8,96,640]{2,1,0:T(8,128)(2,1)S(1)} all-to-all(bf16[8,96,640]{2,1,0:T(8,128)(2,1)S(1)} %reshape.116), channel_id=1, replica_groups=mesh['cfg'=2,'seq'=32,'head'=8] {'head'}, dimensions={0} | all-to-all | bytes 1966080 | tf_op jit(solution)/shard_map/all_to_all | solution.py:90
  181.3 1.1 copy.53
  (14 shorter events, 0.5 us)
Async XLA Ops:
  0.0 58.9 %copy-start = (s32[40,3]{0,1:T(4,128)S(1)}, s32[40,3]{0,1:T(4,128)}, u32[]{:S(2)}) copy-start(s32[40,3]{0,1:T(4,128)} %param.9) | copy-start | bytes 1444
  2.2 23.7 %all-to-all-start.1 = ((bf16[96,8,640]{2,0,1:T(8,128)(2,1)}), bf16[96,8,640]{2,0,1:T(8,128)(2,1)S(1)}, u32[]{:S(2)}, u32[]{:S(2)}) async-start(bf16[96,8,640]{2,0,1:T(8,128)(2,1)} %bitcast.53), calls=%async_computation.1 | async-start | bytes 1966080 | tf_op jit(solution)/shard_map/all_to_all | solution.py:54
  45.1 34.2 %collective-permute-start = (bf16[768,1280]{1,0:T(8,128)(2,1)}, bf16[768,1280]{1,0:T(8,128)(2,1)}, u32[]{:S(2)}, u32[]{:S(2)}) collective-permute-start(bf16[768,1280]{1,0:T(8,128)(2,1)} %pad_maximum_fusion.1), channel_id=1, source_target_pairs={{0,8},{8,16},{16,24},{24,32},{32,40},{40,48},{48,56},{56,64},{64,7... | collective-permute-start | bytes 5898248 | tf_op jit(solution)/shard_map/ppermute | solution.py:19
  51.1 28.3 %collective-permute-start.1 = (bf16[768,1280]{1,0:T(8,128)(2,1)}, bf16[768,1280]{1,0:T(8,128)(2,1)}, u32[]{:S(2)}, u32[]{:S(2)}) collective-permute-start(bf16[768,1280]{1,0:T(8,128)(2,1)} %pad_maximum_fusion.1), channel_id=1, source_target_pairs={{8,0},{16,8},{24,16},{32,24},{40,32},{48,40},{56,48},{64,56},{72,6... | collective-permute-start | bytes 5898248 | tf_op jit(solution)/shard_map/ppermute | solution.py:21
  55.3 19.0 %all-to-all-start = ((bf16[96,8,640]{2,0,1:T(8,128)(2,1)}), bf16[96,8,640]{2,0,1:T(8,128)(2,1)S(1)}, u32[]{:S(2)}, u32[]{:S(2)}) async-start(bf16[96,8,640]{2,0,1:T(8,128)(2,1)} %bitcast.75), calls=%async_computation | async-start | bytes 1966080 | tf_op jit(solution)/shard_map/all_to_all | solution.py:53
  74.2 1.0 copy-start.1
where the time goes:
time: 185 us; the launch traced here: 182 us
  blocking collectives  36.5 us (20%)
  matrix products  35.1 us (19%)
  local copies, waits for them, and re-layouts  30.8 us (17%)
  waiting for transfers between devices  30.2 us (16%)
  other arithmetic  27.6 us (15%)
  starting transfers between devices  18.9 us (10%)
  loops' own time  3.12 us (2%)
    dot_general x5, matrix products, one_head(): lax.dot_general(query_h, key_h, (((1,), (1,)), ((), ())), preferred_eleme...  25.8 us
    all_to_all x1, blocking collectives, shards(): lax.all_to_all(result, 'head', split_axis=0, concat_axis=1, tiled=True)  18.9 us
    all_to_all x1, blocking collectives, shards(): lax.all_to_all(values, 'head', split_axis=1, concat_axis=0, tiled=True)  17.7 us
    concatenate x1, other arithmetic, padded(): jnp.concatenate([lax.ppermute(tail, axis, [(i, (i + 1) % count) for i in...  17.2 us
    all_to_all x1, waiting for transfers between devices, shards(): lax.all_to_all(queries, 'head', split_axis=1, concat_axis=0, tiled=True)  15.3 us
    all_to_all x1, waiting for transfers between devices, shards(): lax.all_to_all(keys, 'head', split_axis=1, concat_axis=0, tiled=True)  15 us
    dot_general x5, matrix products, finish(): mixed = jnp.dot(probs, value_h, preferred_element_type=jnp.float32) / total  9.24 us
    slice x2, local copies, waits for them, and re-layouts, layer_rim_pairs(): extended[:, width:].reshape(3 * lrows, local_heads, HD)  8.81 us
  transfers between devices with their start and end apart: 4, of which 2 were waited for; matrix products, arithmetic and copies ran while one was open for 4% of the time, Pallas kernels for 0%

commit v1 on v0

v1 whole, which is shorter than its diff:
```python
import functools
import math

import jax
import jax.numpy as jnp
from jax import lax
from jax.experimental import pallas as pl
from jax.experimental.pallas import tpu as pltpu
from jax.sharding import PartitionSpec as P

HD = 128
TILE = 384
ROWS = 2
NEAR = 3
TURNS = (6, 5, 7, 4, 2, 1, 3, 0)
ANY = pl.BlockSpec(memory_space=pl.ANY)
SMEM = pl.BlockSpec(memory_space=pltpu.SMEM)
VMEM = pl.BlockSpec(memory_space=pltpu.VMEM)


def column(index):
    return pl.ds(pl.multiple_of(index * HD, HD), HD)


def rank_of(device, slot, count):
    return slot * count + (device if slot % 2 == 0 else count - 1 - device)


def sort_heads(windows, order):
    heads = order.shape[0]

    def kind(head):
        return 3 - 2 * windows[0, head] - windows[1, head]

    def tally(head, counts):
        this = kind(head)
        return tuple(n + (this == i).astype(jnp.int32) for i, n in enumerate(counts))

    zero = jnp.int32(0)
    counts = lax.fori_loop(0, heads, tally, (zero,) * 4)
    starts = (zero, counts[0], counts[0] + counts[1], counts[0] + counts[1] + counts[2])

    def place(head, nexts):
        this = kind(head)
        spot = zero
        for i, n in enumerate(nexts):
            spot = jnp.where(this == i, n, spot)
        order[spot] = head
        return tuple(n + (this == i).astype(jnp.int32) for i, n in enumerate(nexts))

    lax.fori_loop(0, heads, place, starts)


def fetch(arrays, held, sems):
    copies = [
        pltpu.make_async_copy(array, held.at[i], sems.at[i]) for i, array in enumerate(arrays)
    ]
    for copy in copies:
        copy.start()
    return copies


def fill(order, device, devices, held, parts, room):
    at = 0
    for i, slots in parts:
        for slot in slots:
            head = order[rank_of(device, slot, devices)]
            room[at] = held[i, :, column(head)]
            at += 1


def pack_first(near, windows, keys, values, *refs):
    *packed, order, held, room, in_sems, out_sems = refs
    arrivals = fetch((keys, values), held, in_sems)
    sort_heads(windows, order)
    for copy in arrivals:
        copy.wait()
    copies = []
    for turn in TURNS:
        device = lax.axis_index("head") ^ turn
        fill(order, device, len(packed), held, ((0, near), (1, near)), room.at[turn])
        copy = pltpu.make_async_copy(room.at[turn], packed[turn], out_sems.at[turn])
        copy.start()
        copies.append(copy)
    for copy in copies:
        copy.wait()


def pack_second(slots, far, order, queries, keys, values, packed, held, room, in_sems, out_sems):
    arrivals = fetch((queries, keys, values), held, in_sems)
    for copy in arrivals:
        copy.wait()
    copies = []
    devices = packed.shape[0]
    for device in range(devices):
        fill(order, device, devices, held, ((0, slots), (1, far), (2, far)), room.at[device])
        copy = pltpu.make_async_copy(room.at[device], packed.at[device], out_sems.at[device])
        copy.start()
        copies.append(copy)
    for copy in copies:
        copy.wait()


def call_pack(body, scalar, arrays, devices, blocks, out_shape, out_specs, name):
    tokens, model = arrays[0].shape
    return pl.pallas_call(
        body,
        out_shape=out_shape,
        in_specs=[SMEM] + [ANY] * len(arrays),
        out_specs=out_specs,
        scratch_shapes=[
            pltpu.VMEM((len(arrays), tokens, model), jnp.bfloat16),
            pltpu.VMEM((devices, blocks, tokens, HD), jnp.bfloat16),
            pltpu.SemaphoreType.DMA((len(arrays),)),
            pltpu.SemaphoreType.DMA((devices,)),
        ],
        compiler_params=pltpu.CompilerParams(vmem_limit_bytes=16 * 2**20),
        cost_estimate=pl.CostEstimate(
            flops=0, bytes_accessed=4 * devices * blocks * tokens * HD, transcendentals=0
        ),
        name=name,
    )(scalar, *arrays)


def gather(after, *refs):
    *chunks, out, sems = refs
    copies = [
        pltpu.make_async_copy(chunk, out.at[lax.axis_index("head") ^ turn], sems.at[turn])
        for turn, chunk in enumerate(chunks)
    ]
    for copy in copies:
        copy.start()
    for copy in copies:
        copy.wait()


def call_gather(after, chunks, name):
    devices = len(chunks)
    return pl.pallas_call(
        gather,
        out_shape=jax.ShapeDtypeStruct((devices, *chunks[0].shape), chunks[0].dtype),
        in_specs=[ANY] * (devices + 1),
        out_specs=VMEM,
        scratch_shapes=[pltpu.SemaphoreType.DMA((devices,))],
        cost_estimate=pl.CostEstimate(
            flops=0, bytes_accessed=4 * devices * chunks[0].size, transcendentals=0
        ),
        name=name,
    )(after, *chunks)


def unpack(split, order, first, second, out):
    devices = first.shape[0]
    slots = first.shape[1] + second.shape[1]
    for device in range(devices):
        for slot in range(slots):
            array, at = (first, slot) if slot < split else (second, slot - split)
            head = order[rank_of(device, slot, devices)]
            out[:, column(head)] = array[device, at]


def attend(slots, at, has_rim, devices, *refs):
    if has_rim:
        order, windows, queries, own, before, after, out, q, k, v, sems = refs
    else:
        order, windows, queries, own, out, q, k, v, sems = refs
    count = len(slots)
    group, tokens = q.shape[1:3]
    q_at, k_at, v_at = at
    layer, device, layers = lax.axis_index("seq"), lax.axis_index("head"), lax.axis_size("seq")

    def extents(n):
        slot = slots[0] + n
        back = jnp.where(slot % 2 == 0, device, devices - 1 - device)
        head = order[slot * devices + back]
        return windows[0, head], windows[1, head]

    def pair(array, n, part, k_col, v_col):
        chunks = pl.ds(part * group, group)
        return (
            pltpu.make_async_copy(array.at[:, k_col + n], k.at[n, chunks], sems.at[n, 1 + 2 * part]),
            pltpu.make_async_copy(
                array.at[:, v_col + n], v.at[n, chunks, :, pl.ds(0, HD)], sems.at[n, 2 + 2 * part]
            ),
        )

    def own_copies(n):
        mid = 1 if has_rim else 0
        query = pltpu.make_async_copy(queries.at[:, q_at + n], q.at[n], sems.at[n, 0])
        return (query, *pair(own, n, mid, k_at, v_at))

    def near_sides(n):
        far_sight, _ = extents(n)
        return (
            ((far_sight > 0) & (layer > 0), pair(before, n, 0, 0, count)),
            ((far_sight > 0) & (layer < layers - 1), pair(after, n, 2, 0, count)),
        )

    def issue(n, carry):
        for copy in own_copies(n):
            copy.start()
        if has_rim:
            for wanted, copies in near_sides(n):

                @pl.when(wanted)
                def _():
                    for copy in copies:
                        copy.start()

        return carry

    def arrive(n):
        for copy in own_copies(n):
            copy.wait()
        if has_rim:
            for wanted, copies in near_sides(n):

                @pl.when(wanted)
                def _():
                    for copy in copies:
                        copy.wait()

    lax.fori_loop(0, count, issue, 0)
    v[..., HD:] = jnp.ones((*v.shape[:3], HD), v.dtype)
    factor = HD ** (-0.5) * math.log2(math.e)

    def block(n, tile, first, parts, both):
        keep = group if both else group // ROWS
        shift = 0 if both else tile * (group // ROWS)
        spans = [pl.ds((first + part) * group + shift, keep) for part in range(parts)]
        some = group // ROWS // 2
        pieces = [pl.ds(tile * (group // ROWS) + piece * some, some) for piece in range(2)]
        scores = [
            [
                lax.dot_general(
                    q[n, chunks].reshape(some * tokens, HD),
                    k[n, s].reshape(keep * tokens, HD),
                    (((1,), (1,)), ((), ())),
                    preferred_element_type=jnp.float32,
                )
                for s in spans
            ]
            for chunks in pieces
        ]
        for chunks, row in zip(pieces, scores):
            largest = functools.reduce(
                jnp.maximum, [jnp.max(score, axis=1, keepdims=True) for score in row]
            )
            mixed = None
            for s, score in zip(spans, row):
                probs = jnp.exp2((score - largest) * factor).astype(jnp.bfloat16)
                value = v[n, s].reshape(keep * tokens, 2 * HD)
                term = jnp.dot(probs, value, preferred_element_type=jnp.float32)
                mixed = term if mixed is None else mixed + term
            result = mixed[:, :HD] / mixed[:, HD:]
            out[chunks, n] = result.astype(out.dtype).reshape(some, tokens, HD)

    def each(n, carry):
        arrive(n)
        far_sight, both_rows = extents(n)
        if has_rim:
            first = jnp.where(far_sight > 0, jnp.where(layer > 0, 0, 1), 1)
            last = jnp.where(far_sight > 0, jnp.where(layer < layers - 1, 2, 1), 1)
        else:
            first = last = jnp.int32(0)
        parts = last - first + 1
        for both in (False, True):
            for number in (1, 2, 3) if has_rim else (1,):

                @pl.when((parts == number) & ((both_rows > 0) == both))
                def _():
                    def tiles(tile, inner):
                        block(n, tile, first, number, both)
                        return inner

                    lax.fori_loop(0, ROWS, tiles, 0)

        return carry

    lax.fori_loop(0, count, each, 0)


def call_attend(slots, at, order, windows, queries, own, sides, name):
    count = len(slots)
    devices, _, tokens, _ = own.shape
    span = devices * tokens
    parts = 1 + len(sides)
    pairs = count * span * span * parts
    return pl.pallas_call(
        functools.partial(attend, slots, at, bool(sides), devices),
        out_shape=jax.ShapeDtypeStruct((devices, count, tokens, HD), jnp.bfloat16),
        in_specs=[SMEM] * 2 + [ANY] * (2 + len(sides)),
        out_specs=pl.BlockSpec(memory_space=pltpu.VMEM),
        scratch_shapes=[
            pltpu.VMEM((count, devices, tokens, HD), jnp.bfloat16),
            pltpu.VMEM((count, parts * devices, tokens, HD), jnp.bfloat16),
            pltpu.VMEM((count, parts * devices, tokens, 2 * HD), jnp.bfloat16),
            pltpu.SemaphoreType.DMA((count, 7)),
        ],
        compiler_params=pltpu.CompilerParams(vmem_limit_bytes=48 * 2**20),
        cost_estimate=pl.CostEstimate(
            flops=2 * pairs * HD, bytes_accessed=8 * count * span * HD, transcendentals=pairs
        ),
        name=name,
    )(order, windows, queries, own, *sides)


def shards(queries, keys, values, windows):
    tokens, model = queries.shape
    heads = model // HD
    devices = lax.axis_size("head")
    layers = lax.axis_size("seq")
    slots = heads // devices
    near, far = tuple(range(NEAR)), tuple(range(NEAR, slots))
    windows = windows.T
    def moved(number):
        return pl.CostEstimate(
            flops=0, bytes_accessed=4 * number * tokens * HD, transcendentals=0
        )

    def swap(array):
        return lax.all_to_all(array, "head", split_axis=0, concat_axis=0, tiled=True)

    first_blocks, blocks = 2 * len(near), slots + 2 * len(far)
    chunk = jax.ShapeDtypeStruct((first_blocks, tokens, HD), jnp.bfloat16)
    *first, order = call_pack(
        functools.partial(pack_first, near), windows, (keys, values), devices, first_blocks,
        (chunk,) * devices + (jax.ShapeDtypeStruct((heads,), jnp.int32),),
        (ANY,) * devices + (SMEM,), "pack_near_keys_values",
    )
    chunks = list(first)
    for turn in TURNS[:-1]:
        chunks[turn] = lax.ppermute(first[turn], "head", [(i, i ^ turn) for i in range(devices)])
    second = call_pack(
        functools.partial(pack_second, tuple(range(slots)), far), order, (queries, keys, values),
        devices, blocks, jax.ShapeDtypeStruct((devices, blocks, tokens, HD), jnp.bfloat16), ANY,
        "pack_queries_and_rest",
    )
    rest = swap(second)
    near_kv = call_gather(second, chunks, "gather_near_keys_values")

    def neighbours(array):
        ends = layers - 1
        return (
            lax.ppermute(array, "seq", [(i, i + 1) for i in range(ends)]),
            lax.ppermute(array, "seq", [(i + 1, i) for i in range(ends)]),
        )

    sides = neighbours(near_kv)

    def with_far():
        far_sides = neighbours(rest[:, slots:])
        return call_attend(
            far, (NEAR, slots, slots + len(far)), order, windows, rest, rest, far_sides,
            "attend_far_slots_three_layers",
        )

    def without_far():
        return call_attend(
            far, (NEAR, slots, slots + len(far)), order, windows, rest, rest, (),
            "attend_far_slots_own_layer",
        )

    wide = jnp.sum(windows[0]) > NEAR * devices
    far_out = lax.cond(wide, with_far, without_far)
    far_back = swap(far_out)
    near_out = call_attend(
        near, (0, 0, NEAR), order, windows, rest, near_kv, sides, "attend_near_slots"
    )
    near_back = swap(near_out)

    number = slots * devices
    return pl.pallas_call(
        functools.partial(unpack, NEAR),
        out_shape=jax.ShapeDtypeStruct((tokens, model), jnp.bfloat16),
        in_specs=[SMEM, VMEM, VMEM],
        out_specs=VMEM,
        cost_estimate=moved(number),
        name="unpack_attended",
    )(order, near_back, far_back)


def solution(mesh):
    placed = P(("cfg", "seq", "head"), None)
    return jax.shard_map(
        shards,
        mesh=mesh,
        in_specs=(placed, placed, placed, P()),
        out_specs=placed,
        check_vma=False,
    )
```

time: 185 us -> 114 us (0.62)
  the two profiles are of different devices: /device:TPU:1 before, /device:TPU:128 now
where the time goes in v1:
time: 114 us
  starting transfers between devices  45.7 us (40%)
  Pallas kernels  26 us (23%)
  waiting for transfers between devices  19.3 us (17%)
  blocking collectives  17.3 us (15%)
  local copies, waits for them, and re-layouts  3.73 us (3%)
    ppermute x7, starting transfers between devices, shards(): lax.ppermute(first[turn], 'head', [(i, i ^ turn) for i in range(devices)])  28.2 us
    all_to_all x1, blocking collectives, swap(): lax.all_to_all(array, 'head', split_axis=0, concat_axis=0, tiled=True)  17.3 us
    ppermute x7, waiting for transfers between devices, shards(): lax.ppermute(first[turn], 'head', [(i, i ^ turn) for i in range(devices)])  15.3 us
    pallas_call x2, Pallas kernels, call_attend(): pl.pallas_call(functools.partial(attend, slots, at, bool(sides), devices)...  13.2 us
    all_to_all x2, starting transfers between devices, swap(): lax.all_to_all(array, 'head', split_axis=0, concat_axis=0, tiled=True)  10.8 us
    pallas_call x2, Pallas kernels, call_pack(): pl.pallas_call(body, out_shape=out_shape, in_specs=[SMEM] + [ANY] * len(a...  8.03 us
    ppermute x1, starting transfers between devices, neighbours(): lax.ppermute(array, 'seq', [(i + 1, i) for i in range(ends)])  4.85 us
    unnamed x28, local copies, waits for them, and re-layouts  3.73 us
  transfers between devices with their start and end apart: 11, of which 5 were waited for; matrix products, arithmetic and copies ran while one was open for 1% of the time, Pallas kernels for 14%

profile of v1, /device:TPU:128, one launch (start us, length us, event | category | flops | bytes accessed | tf_op | source)
XLA Modules:
  0.0 113.7 jit_solution(7830366042867725325)
XLA Ops:
  0.0 1.2 %copy-done = bf16[96,5120]{1,0:T(8,128)(2,1)S(1)} copy-done((bf16[96,5120]{1,0:T(8,128)(2,1)S(1)}, bf16[96,5120]{1,0:T(8,128)(2,1)}, u32[]{:S(2)}) %copy-start) | copy-done | bytes 983064
  1.2 1.2 %copy-done.1 = bf16[96,5120]{1,0:T(8,128)(2,1)S(1)} copy-done((bf16[96,5120]{1,0:T(8,128)(2,1)S(1)}, bf16[96,5120]{1,0:T(8,128)(2,1)}, u32[]{:S(2)}) %copy-start.1) | copy-done | bytes 983064
  2.4 5.2 %pack_near_keys_values.1 = (bf16[6,96,128]{2,1,0:T(8,128)(2,1)S(1)}, bf16[6,96,128]{2,1,0:T(8,128)(2,1)S(1)}, bf16[6,96,128]{2,1,0:T(8,128)(2,1)S(1)}, bf16[6,96...) custom-call(s32[3,40]{1,0:T(4,128)} %bitcast.1, ...), custom_call_target="tpu_custom_call" | custom-call | bytes 2359296 | tf_op jit(solution)/shard_map/pack_near_keys_values/pallas_call | solution.py:106
  7.6 0.0 copy-start.4
  7.6 0.7 copy-done.4
  8.3 0.0 copy-done.3
  8.3 2.8 %pack_queries_and_rest.1.after = bf16[8,9,96,128]{3,2,1,0:T(8,128)(2,1)} custom-call(s32[40]{0:T(128)S(1)} %get-tuple-element.35.order.refs_0_, bf16[96,5120]{1,0:T(8,128)(2,1)S(1)} %copy-done.3, bf16[96,5120]{1,0:T(8,128)(2,1)S(1)} %copy-done, bf16[96,5120]{1,0:T(8,128)(2,1)S(1)} %copy-done.1), custom_call_target="tpu_custom_call" | custom-call | bytes 3538944 | tf_op jit(solution)/shard_map/pack_queries_and_rest/pallas_call | solution.py:106
  11.1 6.9 %all-to-all-start = ((bf16[8,9,96,128]{3,2,1,0:T(8,128)(2,1)}), bf16[8,9,96,128]{3,2,1,0:T(8,128)(2,1)}, u32[]{:S(2)}, u32[]{:S(2)}) async-start(bf16[8,9,96,128]{3,2,1,0:T(8,128)(2,1)} %pack_queries_and_rest.1.after), calls=%async_computation | async-start | bytes 3538944 | tf_op jit(solution)/shard_map/all_to_all | solution.py:322
  18.1 3.9 %collective-permute-start.2 = (bf16[6,96,128]{2,1,0:T(8,128)(2,1)S(1)}, bf16[6,96,128]{2,1,0:T(8,128)(2,1)S(1)}, u32[]{:S(2)}, u32[]{:S(2)}) collective-permute-start(bf16[6,96,128]{2,1,0:T(8,128)(2,1)S(1)} %get-tuple-element.37), channel_id=1, source_target_pairs={{0,1},{1,0},{2,3},{3,2},{4,5},{5,4},{6,7},{7,6},{8,9},{9,8},{10,11... | collective-permute-start | bytes 442376 | tf_op jit(solution)/shard_map/ppermute | solution.py:333
  22.0 4.6 %collective-permute-start.3 = (bf16[6,96,128]{2,1,0:T(8,128)(2,1)S(1)}, bf16[6,96,128]{2,1,0:T(8,128)(2,1)S(1)}, u32[]{:S(2)}, u32[]{:S(2)}) collective-permute-start(bf16[6,96,128]{2,1,0:T(8,128)(2,1)S(1)} %get-tuple-element.38), channel_id=1, source_target_pairs={{0,2},{1,3},{2,0},{3,1},{4,6},{5,7},{6,4},{7,5},{8,10},{9,11},{10,... | collective-permute-start | bytes 442376 | tf_op jit(solution)/shard_map/ppermute | solution.py:333
  26.6 1.9 %collective-permute-start.4 = (bf16[6,96,128]{2,1,0:T(8,128)(2,1)S(1)}, bf16[6,96,128]{2,1,0:T(8,128)(2,1)S(1)}, u32[]{:S(2)}, u32[]{:S(2)}) collective-permute-start(bf16[6,96,128]{2,1,0:T(8,128)(2,1)S(1)} %get-tuple-element.39), channel_id=1, source_target_pairs={{0,3},{1,2},{2,1},{3,0},{4,7},{5,6},{6,5},{7,4},{8,11},{9,10},{10,... | collective-permute-start | bytes 442376 | tf_op jit(solution)/shard_map/ppermute | solution.py:333
  28.5 5.4 %collective-permute-start.5 = (bf16[6,96,128]{2,1,0:T(8,128)(2,1)S(1)}, bf16[6,96,128]{2,1,0:T(8,128)(2,1)S(1)}, u32[]{:S(2)}, u32[]{:S(2)}) collective-permute-start(bf16[6,96,128]{2,1,0:T(8,128)(2,1)S(1)} %get-tuple-element.40), channel_id=1, source_target_pairs={{0,4},{1,5},{2,6},{3,7},{4,0},{5,1},{6,2},{7,3},{8,12},{9,13},{10,... | collective-permute-start | bytes 442376 | tf_op jit(solution)/shard_map/ppermute | solution.py:333
  33.9 2.2 %collective-permute-start.6 = (bf16[6,96,128]{2,1,0:T(8,128)(2,1)S(1)}, bf16[6,96,128]{2,1,0:T(8,128)(2,1)S(1)}, u32[]{:S(2)}, u32[]{:S(2)}) collective-permute-start(bf16[6,96,128]{2,1,0:T(8,128)(2,1)S(1)} %get-tuple-element.41), channel_id=1, source_target_pairs={{0,5},{1,4},{2,7},{3,6},{4,1},{5,0},{6,3},{7,2},{8,13},{9,12},{10,... | collective-permute-start | bytes 442376 | tf_op jit(solution)/shard_map/ppermute | solution.py:333
  36.1 8.9 %collective-permute-done.2.refs_1_ = bf16[6,96,128]{2,1,0:T(8,128)(2,1)S(1)} collective-permute-done((bf16[6,96,128]{2,1,0:T(8,128)(2,1)S(1)}, bf16[6,96,128]{2,1,0:T(8,128)(2,1)S(1)}, u32[]{:S(2)}, u32[]{:S(2)}) %collective-permute-start.2) | collective-permute-done | bytes 147488 | tf_op jit(solution)/shard_map/ppermute | solution.py:333
  45.0 6.0 %collective-permute-start.7 = (bf16[6,96,128]{2,1,0:T(8,128)(2,1)S(1)}, bf16[6,96,128]{2,1,0:T(8,128)(2,1)S(1)}, u32[]{:S(2)}, u32[]{:S(2)}) collective-permute-start(bf16[6,96,128]{2,1,0:T(8,128)(2,1)S(1)} %get-tuple-element.42), channel_id=1, source_target_pairs={{0,6},{1,7},{2,4},{3,5},{4,2},{5,3},{6,0},{7,1},{8,14},{9,15},{10,... | collective-permute-start | bytes 442376 | tf_op jit(solution)/shard_map/ppermute | solution.py:333
  51.0 0.0 collective-permute-done.3.refs_2_
  51.0 0.0 copy-start.7
  51.0 4.1 %collective-permute-start.8 = (bf16[6,96,128]{2,1,0:T(8,128)(2,1)S(1)}, bf16[6,96,128]{2,1,0:T(8,128)(2,1)S(1)}, u32[]{:S(2)}, u32[]{:S(2)}) collective-permute-start(bf16[6,96,128]{2,1,0:T(8,128)(2,1)S(1)} %get-tuple-element.43), channel_id=1, source_target_pairs={{0,7},{1,6},{2,5},{3,4},{4,3},{5,2},{6,1},{7,0},{8,15},{9,14},{10,... | collective-permute-start | bytes 442376 | tf_op jit(solution)/shard_map/ppermute | solution.py:333
  55.2 0.0 collective-permute-done.4.refs_3_
  55.2 0.0 copy-start.8
  55.2 0.0 collective-permute-done.5.refs_4_
  55.2 0.0 copy-start.9
  55.2 0.0 collective-permute-done.6.refs_5_
  55.2 0.0 copy-start.10
  55.2 1.4 %collective-permute-done.7.refs_6_ = bf16[6,96,128]{2,1,0:T(8,128)(2,1)S(1)} collective-permute-done((bf16[6,96,128]{2,1,0:T(8,128)(2,1)S(1)}, bf16[6,96,128]{2,1,0:T(8,128)(2,1)S(1)}, u32[]{:S(2)}, u32[]{:S(2)}) %collective-permute-start.7) | collective-permute-done | bytes 147488 | tf_op jit(solution)/shard_map/ppermute | solution.py:333
  56.7 5.0 %collective-permute-done.8.refs_7_ = bf16[6,96,128]{2,1,0:T(8,128)(2,1)S(1)} collective-permute-done((bf16[6,96,128]{2,1,0:T(8,128)(2,1)S(1)}, bf16[6,96,128]{2,1,0:T(8,128)(2,1)S(1)}, u32[]{:S(2)}, u32[]{:S(2)}) %collective-permute-start.8) | collective-permute-done | bytes 147488 | tf_op jit(solution)/shard_map/ppermute | solution.py:333
  61.7 0.0 copy-done.6
  61.7 0.0 copy-done.7
  61.7 0.0 copy-done.8
  61.7 0.0 copy-done.9
  61.7 0.0 copy-done.10
  61.7 0.0 copy-done.11
  61.7 0.6 copy-done.12
  62.4 2.4 %gather_near_keys_values.1.refs_3_ = bf16[8,6,96,128]{3,2,1,0:T(8,128)(2,1)} custom-call(bf16[8,9,96,128]{3,2,1,0:T(8,128)(2,1)} %pack_queries_and_rest.1.after, bf16[6,96,128]{2,1,0:T(8,128)(2,1)} %copy-done.4, bf16[6,96,128]{2,1,0:T(8,128)(2,1)} %copy-done.6, bf16[6,96,128]{2,1,0:T(8,128)(2,1)} %copy-done.7, bf16[6,96,128]{2,1,0:T(8,128)(2,1)} %copy-done.8, ...), custom_call_target="tpu_custom_call" | custom-call | bytes 2359296 | tf_op jit(solution)/shard_map/gather_near_keys_values/pallas_call | solution.py:139
  64.8 1.9 %collective-permute-start.9 = (bf16[8,6,96,128]{3,2,1,0:T(8,128)(2,1)}, bf16[8,6,96,128]{3,2,1,0:T(8,128)(2,1)S(1)}, u32[]{:S(2)}, u32[]{:S(2)}) collective-permute-start(bf16[8,6,96,128]{3,2,1,0:T(8,128)(2,1)} %gather_near_keys_values.1.refs_3_), channel_id=1, source_target_pairs={{0,8},{8,16},{16,24},{24,32},{32,40},{40,48},{48,56},{56,64},{64,7... | collective-permute-start | bytes 3538952 | tf_op jit(solution)/shard_map/ppermute | solution.py:345
  66.7 4.9 %collective-permute-start.10 = (bf16[8,6,96,128]{3,2,1,0:T(8,128)(2,1)}, bf16[8,6,96,128]{3,2,1,0:T(8,128)(2,1)}, u32[]{:S(2)}, u32[]{:S(2)}) collective-permute-start(bf16[8,6,96,128]{3,2,1,0:T(8,128)(2,1)} %gather_near_keys_values.1.refs_3_), channel_id=1, source_target_pairs={{8,0},{16,8},{24,16},{32,24},{40,32},{48,40},{56,48},{64,56},{72,6... | collective-permute-start | bytes 3538952 | tf_op jit(solution)/shard_map/ppermute | solution.py:346
  71.6 0.6 slice_reduce_fusion
  72.9 0.0 all-to-all-done.refs_2_
  72.9 4.9 %conditional.1 = (bf16[8,2,96,128]{3,2,1,0:T(8,128)(2,1)}) conditional(s32[]{:T(128)} %convert_element_type.3, (s32[40]{0:T(128)S(1)}, s32[3,40]{1,0:T(4,128)S(1)}, bf16[8,9,96,128]{3,2,1,0:T(8,128)(2,1)}) %tuple.15, (bf16[8,9,96,128]{3,2,1,0:T(8,128)(2,1)}, s32[40]{0:T(128)S(1)}, s32[3,40]{1,0:T(4,128)S(1)}) %tuple.16), branch_computations={%region_1.0_spmd, %region_2.0_spmd} | conditional | flops 905969664 | bytes 9437272 | solution.py:365
  72.9 4.8 %attend_far_slots_own_layer.1 = bf16[8,2,96,128]{3,2,1,0:T(8,128)(2,1)} custom-call(s32[40]{0:T(128)S(1)} %get-tuple-element.20.refs_0_, s32[3,40]{1,0:T(4,128)S(1)} %get-tuple-element.21.refs_1_, bf16[8,9,96,128]{3,2,1,0:T(8,128)(2,1)} %get-tuple-element.22.refs_2_.refs_3_, bf16[8,9,96,128]{3,2,1,0:T(8,128)(2,1)} %get-tuple-element.22.refs_2_.refs_3_), custom_call_target="tpu_custom_call" | custom-call | flops 301989888 | bytes 1572864 | tf_op jit(solution)/shard_map/cond/branch_0_fun/attend_far_slots_own_layer/pallas_call | solution.py:289
  77.8 3.8 %all-to-all-start.2 = ((bf16[8,2,96,128]{3,2,1,0:T(8,128)(2,1)}), bf16[8,2,96,128]{3,2,1,0:T(8,128)(2,1)S(1)}, u32[]{:S(2)}, u32[]{:S(2)}) async-start(bf16[8,2,96,128]{3,2,1,0:T(8,128)(2,1)} %get-tuple-element.44), calls=%async_computation.2 | async-start | bytes 786432 | tf_op jit(solution)/shard_map/all_to_all | solution.py:322
  81.6 2.1 %collective-permute-done.9.refs_4_ = bf16[8,6,96,128]{3,2,1,0:T(8,128)(2,1)S(1)} collective-permute-done((bf16[8,6,96,128]{3,2,1,0:T(8,128)(2,1)}, bf16[8,6,96,128]{3,2,1,0:T(8,128)(2,1)S(1)}, u32[]{:S(2)}, u32[]{:S(2)}) %collective-permute-start.9) | collective-permute-done | bytes 1179680 | tf_op jit(solution)/shard_map/ppermute | solution.py:345
  83.8 1.9 %collective-permute-done.10.refs_5_ = bf16[8,6,96,128]{3,2,1,0:T(8,128)(2,1)} collective-permute-done((bf16[8,6,96,128]{3,2,1,0:T(8,128)(2,1)}, bf16[8,6,96,128]{3,2,1,0:T(8,128)(2,1)}, u32[]{:S(2)}, u32[]{:S(2)}) %collective-permute-start.10) | collective-permute-done | bytes 1179680 | tf_op jit(solution)/shard_map/ppermute | solution.py:346
  85.6 8.4 %attend_near_slots.1 = bf16[8,3,96,128]{3,2,1,0:T(8,128)(2,1)S(1)} custom-call(s32[40]{0:T(128)S(1)} %get-tuple-element.35.order.refs_0_, s32[3,40]{1,0:T(4,128)S(1)} %bitcast.5, bf16[8,9,96,128]{3,2,1,0:T(8,128)(2,1)} %all-to-all-done.refs_2_, bf16[8,6,96,128]{3,2,1,0:T(8,128)(2,1)S(1)} %copy-done.2, ...), custom_call_target="tpu_custom_call" | custom-call | flops 1358954496 | bytes 2359296 | tf_op jit(solution)/shard_map/attend_near_slots/pallas_call | solution.py:289
  94.0 0.0 all-to-all-done.2.second
  94.0 0.0 copy-start.5
  94.0 17.3 %all_to_all.15.first = bf16[8,3,96,128]{3,2,1,0:T(8,128)(2,1)} all-to-all(bf16[8,3,96,128]{3,2,1,0:T(8,128)(2,1)S(1)} %attend_near_slots.1), channel_id=1, replica_groups=mesh['cfg'=2,'seq'=32,'head'=8] {'head'}, dimensions={0} | all-to-all | bytes 1179648 | tf_op jit(solution)/shard_map/all_to_all | solution.py:322
  111.4 2.4 %unpack_attended.1 = bf16[96,5120]{1,0:T(8,128)(2,1)} custom-call(s32[40]{0:T(128)S(1)} %get-tuple-element.35.order.refs_0_, bf16[8,3,96,128]{3,2,1,0:T(8,128)(2,1)} %all_to_all.15.first, bf16[8,2,96,128]{3,2,1,0:T(8,128)(2,1)} %copy-done.5), custom_call_target="tpu_custom_call" | custom-call | bytes 1966080 | tf_op jit(solution)/shard_map/unpack_attended/pallas_call | solution.py:373
  (11 shorter events, 0.0 us)
Async XLA Ops:
  0.0 1.2 %copy-start = (bf16[96,5120]{1,0:T(8,128)(2,1)S(1)}, bf16[96,5120]{1,0:T(8,128)(2,1)}, u32[]{:S(2)}) copy-start(bf16[96,5120]{1,0:T(8,128)(2,1)} %keys.3) | copy-start | bytes 2949124
  1.2 1.2 %copy-start.1 = (bf16[96,5120]{1,0:T(8,128)(2,1)S(1)}, bf16[96,5120]{1,0:T(8,128)(2,1)}, u32[]{:S(2)}) copy-start(bf16[96,5120]{1,0:T(8,128)(2,1)} %values.3) | copy-start | bytes 2949124
  2.4 5.9 %copy-start.3 = (bf16[96,5120]{1,0:T(8,128)(2,1)S(1)}, bf16[96,5120]{1,0:T(8,128)(2,1)}, u32[]{:S(2)}) copy-start(bf16[96,5120]{1,0:T(8,128)(2,1)} %queries.1) | copy-start | bytes 2949124
  7.6 0.7 copy-start.4
  11.1 61.8 %all-to-all-start = ((bf16[8,9,96,128]{3,2,1,0:T(8,128)(2,1)}), bf16[8,9,96,128]{3,2,1,0:T(8,128)(2,1)}, u32[]{:S(2)}, u32[]{:S(2)}) async-start(bf16[8,9,96,128]{3,2,1,0:T(8,128)(2,1)} %pack_queries_and_rest.1.after), calls=%async_computation | async-start | bytes 3538944 | tf_op jit(solution)/shard_map/all_to_all | solution.py:322
  18.1 26.9 %collective-permute-start.2 = (bf16[6,96,128]{2,1,0:T(8,128)(2,1)S(1)}, bf16[6,96,128]{2,1,0:T(8,128)(2,1)S(1)}, u32[]{:S(2)}, u32[]{:S(2)}) collective-permute-start(bf16[6,96,128]{2,1,0:T(8,128)(2,1)S(1)} %get-tuple-element.37), channel_id=1, source_target_pairs={{0,1},{1,0},{2,3},{3,2},{4,5},{5,4},{6,7},{7,6},{8,9},{9,8},{10,11... | collective-permute-start | bytes 442376 | tf_op jit(solution)/shard_map/ppermute | solution.py:333
  22.0 29.0 %collective-permute-start.3 = (bf16[6,96,128]{2,1,0:T(8,128)(2,1)S(1)}, bf16[6,96,128]{2,1,0:T(8,128)(2,1)S(1)}, u32[]{:S(2)}, u32[]{:S(2)}) collective-permute-start(bf16[6,96,128]{2,1,0:T(8,128)(2,1)S(1)} %get-tuple-element.38), channel_id=1, source_target_pairs={{0,2},{1,3},{2,0},{3,1},{4,6},{5,7},{6,4},{7,5},{8,10},{9,11},{10,... | collective-permute-start | bytes 442376 | tf_op jit(solution)/shard_map/ppermute | solution.py:333
  26.6 28.6 %collective-permute-start.4 = (bf16[6,96,128]{2,1,0:T(8,128)(2,1)S(1)}, bf16[6,96,128]{2,1,0:T(8,128)(2,1)S(1)}, u32[]{:S(2)}, u32[]{:S(2)}) collective-permute-start(bf16[6,96,128]{2,1,0:T(8,128)(2,1)S(1)} %get-tuple-element.39), channel_id=1, source_target_pairs={{0,3},{1,2},{2,1},{3,0},{4,7},{5,6},{6,5},{7,4},{8,11},{9,10},{10,... | collective-permute-start | bytes 442376 | tf_op jit(solution)/shard_map/ppermute | solution.py:333
  28.5 26.7 %collective-permute-start.5 = (bf16[6,96,128]{2,1,0:T(8,128)(2,1)S(1)}, bf16[6,96,128]{2,1,0:T(8,128)(2,1)S(1)}, u32[]{:S(2)}, u32[]{:S(2)}) collective-permute-start(bf16[6,96,128]{2,1,0:T(8,128)(2,1)S(1)} %get-tuple-element.40), channel_id=1, source_target_pairs={{0,4},{1,5},{2,6},{3,7},{4,0},{5,1},{6,2},{7,3},{8,12},{9,13},{10,... | collective-permute-start | bytes 442376 | tf_op jit(solution)/shard_map/ppermute | solution.py:333
  33.9 21.3 %collective-permute-start.6 = (bf16[6,96,128]{2,1,0:T(8,128)(2,1)S(1)}, bf16[6,96,128]{2,1,0:T(8,128)(2,1)S(1)}, u32[]{:S(2)}, u32[]{:S(2)}) collective-permute-start(bf16[6,96,128]{2,1,0:T(8,128)(2,1)S(1)} %get-tuple-element.41), channel_id=1, source_target_pairs={{0,5},{1,4},{2,7},{3,6},{4,1},{5,0},{6,3},{7,2},{8,13},{9,12},{10,... | collective-permute-start | bytes 442376 | tf_op jit(solution)/shard_map/ppermute | solution.py:333
  45.0 16.7 %copy-start.6 = (bf16[6,96,128]{2,1,0:T(8,128)(2,1)}, bf16[6,96,128]{2,1,0:T(8,128)(2,1)S(1)}, u32[]{:S(2)}) copy-start(bf16[6,96,128]{2,1,0:T(8,128)(2,1)S(1)} %collective-permute-done.2.refs_1_) | copy-start | bytes 442372
  45.0 11.7 %collective-permute-start.7 = (bf16[6,96,128]{2,1,0:T(8,128)(2,1)S(1)}, bf16[6,96,128]{2,1,0:T(8,128)(2,1)S(1)}, u32[]{:S(2)}, u32[]{:S(2)}) collective-permute-start(bf16[6,96,128]{2,1,0:T(8,128)(2,1)S(1)} %get-tuple-element.42), channel_id=1, source_target_pairs={{0,6},{1,7},{2,4},{3,5},{4,2},{5,3},{6,0},{7,1},{8,14},{9,15},{10,... | collective-permute-start | bytes 442376 | tf_op jit(solution)/shard_map/ppermute | solution.py:333
  51.0 10.7 %copy-start.7 = (bf16[6,96,128]{2,1,0:T(8,128)(2,1)}, bf16[6,96,128]{2,1,0:T(8,128)(2,1)S(1)}, u32[]{:S(2)}) copy-start(bf16[6,96,128]{2,1,0:T(8,128)(2,1)S(1)} %collective-permute-done.3.refs_2_) | copy-start | bytes 442372
  51.0 10.7 %collective-permute-start.8 = (bf16[6,96,128]{2,1,0:T(8,128)(2,1)S(1)}, bf16[6,96,128]{2,1,0:T(8,128)(2,1)S(1)}, u32[]{:S(2)}, u32[]{:S(2)}) collective-permute-start(bf16[6,96,128]{2,1,0:T(8,128)(2,1)S(1)} %get-tuple-element.43), channel_id=1, source_target_pairs={{0,7},{1,6},{2,5},{3,4},{4,3},{5,2},{6,1},{7,0},{8,15},{9,14},{10,... | collective-permute-start | bytes 442376 | tf_op jit(solution)/shard_map/ppermute | solution.py:333
  55.2 6.5 %copy-start.8 = (bf16[6,96,128]{2,1,0:T(8,128)(2,1)}, bf16[6,96,128]{2,1,0:T(8,128)(2,1)S(1)}, u32[]{:S(2)}) copy-start(bf16[6,96,128]{2,1,0:T(8,128)(2,1)S(1)} %collective-permute-done.4.refs_3_) | copy-start | bytes 442372
  55.2 6.5 %copy-start.9 = (bf16[6,96,128]{2,1,0:T(8,128)(2,1)}, bf16[6,96,128]{2,1,0:T(8,128)(2,1)S(1)}, u32[]{:S(2)}) copy-start(bf16[6,96,128]{2,1,0:T(8,128)(2,1)S(1)} %collective-permute-done.5.refs_4_) | copy-start | bytes 442372
  55.2 6.5 %copy-start.10 = (bf16[6,96,128]{2,1,0:T(8,128)(2,1)}, bf16[6,96,128]{2,1,0:T(8,128)(2,1)S(1)}, u32[]{:S(2)}) copy-start(bf16[6,96,128]{2,1,0:T(8,128)(2,1)S(1)} %collective-permute-done.6.refs_5_) | copy-start | bytes 442372
  56.6 5.1 %copy-start.11 = (bf16[6,96,128]{2,1,0:T(8,128)(2,1)}, bf16[6,96,128]{2,1,0:T(8,128)(2,1)S(1)}, u32[]{:S(2)}) copy-start(bf16[6,96,128]{2,1,0:T(8,128)(2,1)S(1)} %collective-permute-done.7.refs_6_) | copy-start | bytes 442372
  61.7 0.7 copy-start.12
  62.4 9.2 %copy-start.13 = (s32[40,3]{0,1:T(4,128)S(1)}, s32[40,3]{0,1:T(4,128)}, u32[]{:S(2)}) copy-start(s32[40,3]{0,1:T(4,128)} %param.9) | copy-start | bytes 1444
  64.8 18.9 %collective-permute-start.9 = (bf16[8,6,96,128]{3,2,1,0:T(8,128)(2,1)}, bf16[8,6,96,128]{3,2,1,0:T(8,128)(2,1)S(1)}, u32[]{:S(2)}, u32[]{:S(2)}) collective-permute-start(bf16[8,6,96,128]{3,2,1,0:T(8,128)(2,1)} %gather_near_keys_values.1.refs_3_), channel_id=1, source_target_pairs={{0,8},{8,16},{16,24},{24,32},{32,40},{40,48},{48,56},{56,64},{64,7... | collective-permute-start | bytes 3538952 | tf_op jit(solution)/shard_map/ppermute | solution.py:345
  66.7 18.9 %collective-permute-start.10 = (bf16[8,6,96,128]{3,2,1,0:T(8,128)(2,1)}, bf16[8,6,96,128]{3,2,1,0:T(8,128)(2,1)}, u32[]{:S(2)}, u32[]{:S(2)}) collective-permute-start(bf16[8,6,96,128]{3,2,1,0:T(8,128)(2,1)} %gather_near_keys_values.1.refs_3_), channel_id=1, source_target_pairs={{8,0},{16,8},{24,16},{32,24},{40,32},{48,40},{56,48},{64,56},{72,6... | collective-permute-start | bytes 3538952 | tf_op jit(solution)/shard_map/ppermute | solution.py:346
  72.9 12.7 %copy-start.2 = (bf16[8,6,96,128]{3,2,1,0:T(8,128)(2,1)S(1)}, bf16[8,6,96,128]{3,2,1,0:T(8,128)(2,1)}, u32[]{:S(2)}) copy-start(bf16[8,6,96,128]{3,2,1,0:T(8,128)(2,1)} %gather_near_keys_values.1.refs_3_) | copy-start | bytes 3538948
  77.8 16.2 %all-to-all-start.2 = ((bf16[8,2,96,128]{3,2,1,0:T(8,128)(2,1)}), bf16[8,2,96,128]{3,2,1,0:T(8,128)(2,1)S(1)}, u32[]{:S(2)}, u32[]{:S(2)}) async-start(bf16[8,2,96,128]{3,2,1,0:T(8,128)(2,1)} %get-tuple-element.44), calls=%async_computation.2 | async-start | bytes 786432 | tf_op jit(solution)/shard_map/all_to_all | solution.py:322
  94.0 17.4 %copy-start.5 = (bf16[8,2,96,128]{3,2,1,0:T(8,128)(2,1)}, bf16[8,2,96,128]{3,2,1,0:T(8,128)(2,1)S(1)}, u32[]{:S(2)}) copy-start(bf16[8,2,96,128]{3,2,1,0:T(8,128)(2,1)S(1)} %all-to-all-done.2.second) | copy-start | bytes 1179652

commit v2 on v0

v2 whole, which is shorter than its diff:
```python
import functools
import math

import jax
import jax.numpy as jnp
from jax import lax
from jax.experimental import pallas as pl
from jax.experimental.pallas import tpu as pltpu
from jax.sharding import PartitionSpec as P

HD = 128
TILE = 384
ROWS = 2
NEAR = 3
ANY = pl.BlockSpec(memory_space=pl.ANY)
SMEM = pl.BlockSpec(memory_space=pltpu.SMEM)
VMEM = pl.BlockSpec(memory_space=pltpu.VMEM)


def column(index):
    return pl.ds(pl.multiple_of(index * HD, HD), HD)


def rank_of(device, slot, count):
    return slot * count + (device if slot % 2 == 0 else count - 1 - device)


def sort_heads(windows, order):
    heads = order.shape[0]

    def kind(head):
        return 3 - 2 * windows[0, head] - windows[1, head]

    def tally(head, counts):
        this = kind(head)
        return tuple(n + (this == i).astype(jnp.int32) for i, n in enumerate(counts))

    zero = jnp.int32(0)
    counts = lax.fori_loop(0, heads, tally, (zero,) * 4)
    starts = (zero, counts[0], counts[0] + counts[1], counts[0] + counts[1] + counts[2])

    def place(head, nexts):
        this = kind(head)
        spot = zero
        for i, n in enumerate(nexts):
            spot = jnp.where(this == i, n, spot)
        order[spot] = head
        return tuple(n + (this == i).astype(jnp.int32) for i, n in enumerate(nexts))

    lax.fori_loop(0, heads, place, starts)


def pack(order, parts, packed):
    devices = packed.shape[0]
    for device in range(devices):
        at = 0
        for array, slots in parts:
            for slot in slots:
                head = order[rank_of(device, slot, devices)]
                packed[device, at] = array[:, column(head)]
                at += 1


def pack_first(near, windows, keys, values, packed, order):
    sort_heads(windows, order)
    pack(order, ((keys, near), (values, near)), packed)


def pack_second(slots, far, order, queries, keys, values, packed):
    pack(order, ((queries, slots), (keys, far), (values, far)), packed)


def unpack(order, blocks, out):
    devices, slots = blocks.shape[:2]
    for device in range(devices):
        for slot in range(slots):
            head = order[rank_of(device, slot, devices)]
            out[:, column(head)] = blocks[device, slot]


def attend(near, slots, wide, order, windows, rest, near_kv, *refs):
    *sides, out, q, k, v, sems = refs
    devices, tokens = q.shape[1:3]
    far = slots - near
    layer, device, layers = lax.axis_index("seq"), lax.axis_index("head"), lax.axis_size("seq")

    def extents(n):
        back = jnp.where(n % 2 == 0, device, devices - 1 - device)
        head = order[n * devices + back]
        return windows[0, head], windows[1, head]

    def pair(n, part, array, k_at, v_at):
        chunks = pl.ds(part * devices, devices)
        return (
            pltpu.make_async_copy(array.at[:, k_at], k.at[n, chunks], sems.at[n, 1 + 2 * part]),
            pltpu.make_async_copy(
                array.at[:, v_at], v.at[n, chunks, :, pl.ds(0, HD)], sems.at[n, 2 + 2 * part]
            ),
        )

    def own_copies(n):
        query = pltpu.make_async_copy(rest.at[:, n], q.at[n], sems.at[n, 0])
        if n < near:
            return (query, *pair(n, 1, near_kv, n, near + n))
        return (query, *pair(n, 1, rest, slots + n - near, slots + far + n - near))

    def side_copies(n):
        sight, _ = extents(n)
        if n < near:
            arrays, k_at, v_at = sides[:2], n, near + n
        elif wide:
            arrays, k_at, v_at = sides[2:], n - near, far + n - near
        else:
            return ()
        return (
            ((sight > 0) & (layer > 0), pair(n, 0, arrays[0], k_at, v_at)),
            ((sight > 0) & (layer < layers - 1), pair(n, 2, arrays[1], k_at, v_at)),
        )

    def each_copy(n, act):
        for copy in own_copies(n):
            act(copy)
        for wanted, copies in side_copies(n):

            @pl.when(wanted)
            def _():
                for copy in copies:
                    act(copy)

    for n in range(slots):
        each_copy(n, lambda copy: copy.start())
    v[..., HD:] = jnp.ones((*v.shape[:3], HD), v.dtype)
    factor = HD ** (-0.5) * math.log2(math.e)

    def block(n, tile, first, parts, both):
        half = devices // ROWS
        keep = devices if both else half
        shift = 0 if both else tile * half
        spans = [pl.ds((first + part) * devices + shift, keep) for part in range(parts)]
        query = q[n, pl.ds(tile * half, half)].reshape(half * tokens, HD)
        scores = [
            lax.dot_general(
                query,
                k[n, s].reshape(keep * tokens, HD),
                (((1,), (1,)), ((), ())),
                preferred_element_type=jnp.float32,
            )
            for s in spans
        ]
        largest = functools.reduce(
            jnp.maximum, [jnp.max(score, axis=1, keepdims=True) for score in scores]
        )
        mixed = None
        for s, score in zip(spans, scores):
            probs = jnp.exp2((score - largest) * factor).astype(jnp.bfloat16)
            value = v[n, s].reshape(keep * tokens, 2 * HD)
            term = jnp.dot(probs, value, preferred_element_type=jnp.float32)
            mixed = term if mixed is None else mixed + term
        result = mixed[:, :HD] / mixed[:, HD:]
        out[pl.ds(tile * half, half), n] = result.astype(out.dtype).reshape(half, tokens, HD)

    def each(n, carry):
        for i in range(slots):

            @pl.when(n == i)
            def _():
                each_copy(i, lambda copy: copy.wait())

        sight, rows = extents(n)
        first = jnp.where((sight > 0) & (layer > 0), 0, 1)
        last = jnp.where((sight > 0) & (layer < layers - 1), 2, 1)
        parts = last - first + 1
        for both in (False, True):
            for number in (1, 2, 3):

                @pl.when((parts == number) & ((rows > 0) == both))
                def _():
                    def tiles(tile, inner):
                        block(n, tile, first, number, both)
                        return inner

                    lax.fori_loop(0, ROWS, tiles, 0)

        return carry

    lax.fori_loop(0, slots, each, 0)


def call_attend(near, slots, order, windows, rest, near_kv, sides, name):
    devices, _, tokens, _ = rest.shape
    span = devices * tokens
    pairs = slots * span * span * 2
    return pl.pallas_call(
        functools.partial(attend, near, slots, len(sides) > 2),
        out_shape=jax.ShapeDtypeStruct((devices, slots, tokens, HD), jnp.bfloat16),
        in_specs=[SMEM] * 2 + [ANY] * (2 + len(sides)),
        out_specs=VMEM,
        scratch_shapes=[
            pltpu.VMEM((slots, devices, tokens, HD), jnp.bfloat16),
            pltpu.VMEM((slots, 3 * devices, tokens, HD), jnp.bfloat16),
            pltpu.VMEM((slots, 3 * devices, tokens, 2 * HD), jnp.bfloat16),
            pltpu.SemaphoreType.DMA((slots, 7)),
        ],
        compiler_params=pltpu.CompilerParams(vmem_limit_bytes=48 * 2**20),
        cost_estimate=pl.CostEstimate(
            flops=4 * pairs * HD, bytes_accessed=16 * slots * span * HD, transcendentals=pairs
        ),
        name=name,
    )(order, windows, rest, near_kv, *sides)


def shards(queries, keys, values, windows):
    tokens, model = queries.shape
    heads = model // HD
    devices = lax.axis_size("head")
    layers = lax.axis_size("seq")
    slots = heads // devices
    near, far = tuple(range(NEAR)), tuple(range(NEAR, slots))
    windows = windows.T

    def packed(blocks):
        return jax.ShapeDtypeStruct((devices, blocks, tokens, HD), jnp.bfloat16)

    def moved(blocks):
        return pl.CostEstimate(
            flops=0, bytes_accessed=4 * devices * blocks * tokens * HD, transcendentals=0
        )

    def swap(array):
        return lax.all_to_all(array, "head", split_axis=0, concat_axis=0, tiled=True)

    def neighbours(array):
        ends = layers - 1
        return (
            lax.ppermute(array, "seq", [(i, i + 1) for i in range(ends)]),
            lax.ppermute(array, "seq", [(i + 1, i) for i in range(ends)]),
        )

    blocks = 2 * len(near)
    first, order = pl.pallas_call(
        functools.partial(pack_first, near),
        out_shape=(packed(blocks), jax.ShapeDtypeStruct((heads,), jnp.int32)),
        in_specs=[SMEM, VMEM, VMEM],
        out_specs=(VMEM, SMEM),
        cost_estimate=moved(blocks),
        name="pack_near_keys_values",
    )(windows, keys, values)
    near_kv = swap(first)

    blocks = slots + 2 * len(far)
    second = pl.pallas_call(
        functools.partial(pack_second, tuple(range(slots)), far),
        out_shape=packed(blocks),
        in_specs=[SMEM, VMEM, VMEM, VMEM],
        out_specs=VMEM,
        cost_estimate=moved(blocks),
        name="pack_queries_and_rest",
    )(order, queries, keys, values)
    sides = neighbours(near_kv)
    rest = swap(second)

    def with_far():
        return call_attend(
            NEAR, slots, order, windows, rest, near_kv, (*sides, *neighbours(rest[:, slots:])),
            "attend_all_slots_wide",
        )

    def without_far():
        return call_attend(
            NEAR, slots, order, windows, rest, near_kv, sides, "attend_near_slots_wide"
        )

    wide = jnp.sum(windows[0]) > NEAR * devices
    attended = swap(lax.cond(wide, with_far, without_far))

    return pl.pallas_call(
        unpack,
        out_shape=jax.ShapeDtypeStruct((tokens, model), jnp.bfloat16),
        in_specs=[SMEM, VMEM],
        out_specs=VMEM,
        cost_estimate=moved(slots),
        name="unpack_attended",
    )(order, attended)


def solution(mesh):
    placed = P(("cfg", "seq", "head"), None)
    return jax.shard_map(
        shards,
        mesh=mesh,
        in_specs=(placed, placed, placed, P()),
        out_specs=placed,
        check_vma=False,
    )
```

time: 185 us -> 98.6 us (0.53); the launches traced: 182 us -> 98.2 us
  matrix products: 35.1 us -> 0 us
  local copies, waits for them, and re-layouts: 30.8 us -> 0.01 us
  other arithmetic: 27.6 us -> 0.63 us
  Pallas kernels: 0 us -> 24.6 us
  blocking collectives: 36.5 us -> 22 us
  loops' own time: 3.12 us -> 0.23 us
  waiting for transfers between devices: 30.2 us -> 32.7 us
    dot_general x10 -> x0, matrix products: 35.1 us -> none  [the longest x5 25.8 us: one_head(): lax.dot_general(query_h, key_h, (((1,), (1,)), ((), ())), preferred_eleme...]
    pallas_call x0 -> x4, Pallas kernels: none -> 24.6 us  [the longest x1 14.6 us: call_attend(): pl.pallas_call(functools.partial(attend, near, slots, len(sides) > 2), ou...]
    concatenate x2 -> x0, other arithmetic: 18.7 us -> none  [the longest x1 17.2 us: padded(): jnp.concatenate([lax.ppermute(tail, axis, [(i, (i + 1) % count) for i in...]
    slice x8 -> x0, local copies, waits for them, and re-layouts: 15.3 us -> none  [the longest x2 8.81 us: layer_rim_pairs(): extended[:, width:].reshape(3 * lrows, local_heads, HD)]
    all_to_all x2 -> x1, blocking collectives: 36.5 us -> 22 us  [swap(): lax.all_to_all(array, 'head', split_axis=0, concat_axis=0, tiled=True)]
    all_to_all x7 -> x0, local copies, waits for them, and re-layouts: 12.2 us -> none  [the longest x2 4.53 us: shards(): lax.all_to_all(queries, 'head', split_axis=1, concat_axis=0, tiled=True)]
    reduce_sum x5 -> x1, other arithmetic: 5.43 us -> 0.63 us  [shards(): wide = jnp.sum(windows[0]) > NEAR * devices]
    le x5 -> x0, other arithmetic: 3.51 us -> none  [finish(): lay_gap[None, :] <= extent[0]]
  transfers between devices with their start and end apart: 4 -> 4, of which waited for: 2 -> 2; matrix products, arithmetic and copies ran while one was open for 4% -> 1% of each run, Pallas kernels for 0% -> 4%
where the time goes in v2:
time: 98.6 us; the launch traced here: 98.2 us
  waiting for transfers between devices  32.7 us (33%)
  Pallas kernels  24.6 us (25%)
  blocking collectives  22 us (22%)
  starting transfers between devices  17.3 us (18%)
    all_to_all x2, waiting for transfers between devices, swap(): lax.all_to_all(array, 'head', split_axis=0, concat_axis=0, tiled=True)  32.7 us
    all_to_all x1, blocking collectives, swap(): lax.all_to_all(array, 'head', split_axis=0, concat_axis=0, tiled=True)  22 us
    pallas_call x1, Pallas kernels, call_attend(): pl.pallas_call(functools.partial(attend, near, slots, len(sides) > 2), ou...  14.6 us
    all_to_all x2, starting transfers between devices, swap(): lax.all_to_all(array, 'head', split_axis=0, concat_axis=0, tiled=True)  11.1 us
    pallas_call x1, Pallas kernels, shards(): pl.pallas_call(functools.partial(pack_first, near), out_shape=(packed(blo...  4.07 us
    pallas_call x1, Pallas kernels, shards(): pl.pallas_call(functools.partial(pack_second, tuple(range(slots)), far),...  3.48 us
    ppermute x1, starting transfers between devices, neighbours(): lax.ppermute(array, 'seq', [(i, i + 1) for i in range(ends)])  3.44 us
    ppermute x1, starting transfers between devices, neighbours(): lax.ppermute(array, 'seq', [(i + 1, i) for i in range(ends)])  2.76 us
  transfers between devices with their start and end apart: 4, of which 2 were waited for; matrix products, arithmetic and copies ran while one was open for 1% of the time, Pallas kernels for 4%

profile of v2, /device:TPU:1, one launch (start us, length us, event | category | flops | bytes accessed | tf_op | source)
XLA Modules:
  0.0 98.2 jit_solution(12449279369179762365)
XLA Ops:
  0.0 4.1 %pack_near_keys_values.1 = (bf16[8,6,96,128]{3,2,1,0:T(8,128)(2,1)}, s32[40]{0:T(128)S(1)}) custom-call(s32[3,40]{1,0:T(4,128)} %bitcast.1, bf16[96,5120]{1,0:T(8,128)(2,1)} %keys.3, bf16[96,5120]{1,0:T(8,128)(2,1)} %values.3), custom_call_target="tpu_custom_call" | custom-call | bytes 2359296 | tf_op jit(solution)/shard_map/pack_near_keys_values/pallas_call | solution.py:240
  4.1 7.5 %all-to-all-start.1 = ((bf16[8,6,96,128]{3,2,1,0:T(8,128)(2,1)}), bf16[8,6,96,128]{3,2,1,0:T(8,128)(2,1)S(1)}, u32[]{:S(2)}, u32[]{:S(2)}) async-start(bf16[8,6,96,128]{3,2,1,0:T(8,128)(2,1)} %get-tuple-element.47), calls=%async_computation.1 | async-start | bytes 2359296 | tf_op jit(solution)/shard_map/all_to_all | solution.py:230
  11.6 3.5 %pack_queries_and_rest.1 = bf16[8,9,96,128]{3,2,1,0:T(8,128)(2,1)} custom-call(s32[40]{0:T(128)S(1)} %get-tuple-element.46.order, bf16[96,5120]{1,0:T(8,128)(2,1)} %queries.1, bf16[96,5120]{1,0:T(8,128)(2,1)} %keys.3, bf16[96,5120]{1,0:T(8,128)(2,1)} %values.3), custom_call_target="tpu_custom_call" | custom-call | bytes 3538944 | tf_op jit(solution)/shard_map/pack_queries_and_rest/pallas_call | solution.py:251
  15.1 0.0 copy-start
  15.1 15.2 %all-to-all-done.1 = bf16[8,6,96,128]{3,2,1,0:T(8,128)(2,1)S(1)} async-done(((bf16[8,6,96,128]{3,2,1,0:T(8,128)(2,1)}), bf16[8,6,96,128]{3,2,1,0:T(8,128)(2,1)S(1)}, u32[]{:S(2)}, u32[]{:S(2)}) %all-to-all-start.1) | async-done | bytes 1179680 | tf_op jit(solution)/shard_map/all_to_all | solution.py:230
  30.3 3.6 %all-to-all-start = ((bf16[8,9,96,128]{3,2,1,0:T(8,128)(2,1)}), bf16[8,9,96,128]{3,2,1,0:T(8,128)(2,1)S(1)}, u32[]{:S(2)}, u32[]{:S(2)}) async-start(bf16[8,9,96,128]{3,2,1,0:T(8,128)(2,1)} %pack_queries_and_rest.1), calls=%async_computation | async-start | bytes 3538944 | tf_op jit(solution)/shard_map/all_to_all | solution.py:230
  33.9 2.8 %collective-permute-start.3 = (bf16[8,6,96,128]{3,2,1,0:T(8,128)(2,1)S(1)}, bf16[8,6,96,128]{3,2,1,0:T(8,128)(2,1)}, u32[]{:S(2)}, u32[]{:S(2)}) collective-permute-start(bf16[8,6,96,128]{3,2,1,0:T(8,128)(2,1)S(1)} %all-to-all-done.1), channel_id=1, source_target_pairs={{8,0},{16,8},{24,16},{32,24},{40,32},{48,40},{56,48},{64,56},{72,6... | collective-permute-start | bytes 3538952 | tf_op jit(solution)/shard_map/ppermute | solution.py:236
  36.6 3.4 %collective-permute-start.2 = (bf16[8,6,96,128]{3,2,1,0:T(8,128)(2,1)S(1)}, bf16[8,6,96,128]{3,2,1,0:T(8,128)(2,1)}, u32[]{:S(2)}, u32[]{:S(2)}) collective-permute-start(bf16[8,6,96,128]{3,2,1,0:T(8,128)(2,1)S(1)} %all-to-all-done.1), channel_id=1, source_target_pairs={{0,8},{8,16},{16,24},{24,32},{32,40},{40,48},{48,56},{56,64},{64,7... | collective-permute-start | bytes 3538952 | tf_op jit(solution)/shard_map/ppermute | solution.py:235
  40.1 0.0 copy-done
  40.1 0.6 slice_reduce_fusion
  41.4 17.5 %all-to-all-done = bf16[8,9,96,128]{3,2,1,0:T(8,128)(2,1)S(1)} async-done(((bf16[8,9,96,128]{3,2,1,0:T(8,128)(2,1)}), bf16[8,9,96,128]{3,2,1,0:T(8,128)(2,1)S(1)}, u32[]{:S(2)}, u32[]{:S(2)}) %all-to-all-start) | async-done | bytes 1769504 | tf_op jit(solution)/shard_map/all_to_all | solution.py:230
  58.9 0.0 collective-permute-done.3
  58.9 0.0 collective-permute-done.2
  58.9 14.9 %conditional.1 = (bf16[8,5,96,128]{3,2,1,0:T(8,128)(2,1)}) conditional(s32[]{:T(128)} %convert_element_type.3, (s32[40]{0:T(128)S(1)}, s32[3,40]{1,0:T(4,128)S(1)}, bf16[8,9,96,128]{3,2,1,0:T(8,128)(2,1)S(1)}, bf16[8,6,96,128]{3,2,1,0:T(8,128)(2,1)S(1)}, bf16[8,6,96,128]{3,2,1,0:T(8,128)(2,1)}, ...), branch_computations={%region_1.0_spmd, %region_2.0_spmd} | conditional | flops 3019898880 | bytes 15728728 | solution.py:274
  58.9 14.6 %attend_near_slots_wide.1 = bf16[8,5,96,128]{3,2,1,0:T(8,128)(2,1)} custom-call(s32[40]{0:T(128)S(1)} %get-tuple-element.32.order, s32[3,40]{1,0:T(4,128)S(1)} %get-tuple-element.33.windows, bf16[8,9,96,128]{3,2,1,0:T(8,128)(2,1)S(1)} %get-tuple-element.34.rest, bf16[8,6,96,128]{3,2,1,0:T(8,128)(2,1)S(1)} %get-tuple-element.35.near_kv, ...), custom_call_target="tpu_custom_call" | custom-call | flops 3019898880 | bytes 7864320 | tf_op jit(solution)/shard_map/cond/branch_0_fun/attend_near_slots_wide/pallas_call | solution.py:193
  73.7 22.0 %all_to_all.15.blocks = bf16[8,5,96,128]{3,2,1,0:T(8,128)(2,1)} all-to-all(bf16[8,5,96,128]{3,2,1,0:T(8,128)(2,1)} %get-tuple-element.48), channel_id=1, replica_groups=mesh['cfg'=2,'seq'=32,'head'=8] {'head'}, dimensions={0} | all-to-all | bytes 1966080 | tf_op jit(solution)/shard_map/all_to_all | solution.py:230
  95.8 2.4 %unpack_attended.1 = bf16[96,5120]{1,0:T(8,128)(2,1)} custom-call(s32[40]{0:T(128)S(1)} %get-tuple-element.46.order, bf16[8,5,96,128]{3,2,1,0:T(8,128)(2,1)} %all_to_all.15.blocks), custom_call_target="tpu_custom_call" | custom-call | bytes 1966080 | tf_op jit(solution)/shard_map/unpack_attended/pallas_call | solution.py:276
Async XLA Ops:
  4.1 26.2 %all-to-all-start.1 = ((bf16[8,6,96,128]{3,2,1,0:T(8,128)(2,1)}), bf16[8,6,96,128]{3,2,1,0:T(8,128)(2,1)S(1)}, u32[]{:S(2)}, u32[]{:S(2)}) async-start(bf16[8,6,96,128]{3,2,1,0:T(8,128)(2,1)} %get-tuple-element.47), calls=%async_computation.1 | async-start | bytes 2359296 | tf_op jit(solution)/shard_map/all_to_all | solution.py:230
  15.1 25.1 %copy-start = (s32[40,3]{0,1:T(4,128)S(1)}, s32[40,3]{0,1:T(4,128)}, u32[]{:S(2)}) copy-start(s32[40,3]{0,1:T(4,128)} %param.9) | copy-start | bytes 1444
  30.3 28.6 %all-to-all-start = ((bf16[8,9,96,128]{3,2,1,0:T(8,128)(2,1)}), bf16[8,9,96,128]{3,2,1,0:T(8,128)(2,1)S(1)}, u32[]{:S(2)}, u32[]{:S(2)}) async-start(bf16[8,9,96,128]{3,2,1,0:T(8,128)(2,1)} %pack_queries_and_rest.1), calls=%async_computation | async-start | bytes 3538944 | tf_op jit(solution)/shard_map/all_to_all | solution.py:230
  33.9 25.0 %collective-permute-start.3 = (bf16[8,6,96,128]{3,2,1,0:T(8,128)(2,1)S(1)}, bf16[8,6,96,128]{3,2,1,0:T(8,128)(2,1)}, u32[]{:S(2)}, u32[]{:S(2)}) collective-permute-start(bf16[8,6,96,128]{3,2,1,0:T(8,128)(2,1)S(1)} %all-to-all-done.1), channel_id=1, source_target_pairs={{8,0},{16,8},{24,16},{32,24},{40,32},{48,40},{56,48},{64,56},{72,6... | collective-permute-start | bytes 3538952 | tf_op jit(solution)/shard_map/ppermute | solution.py:236
  36.6 22.2 %collective-permute-start.2 = (bf16[8,6,96,128]{3,2,1,0:T(8,128)(2,1)S(1)}, bf16[8,6,96,128]{3,2,1,0:T(8,128)(2,1)}, u32[]{:S(2)}, u32[]{:S(2)}) collective-permute-start(bf16[8,6,96,128]{3,2,1,0:T(8,128)(2,1)S(1)} %all-to-all-done.1), channel_id=1, source_target_pairs={{0,8},{8,16},{16,24},{24,32},{32,40},{40,48},{48,56},{56,64},{64,7... | collective-permute-start | bytes 3538952 | tf_op jit(solution)/shard_map/ppermute | solution.py:235

commit v3 on v2

--- a/solution.py
+++ b/solution.py
@@ -11,6 +11,7 @@
 HD = 128
 TILE = 384
 ROWS = 2
+PIECES = 2
 NEAR = 3
 ANY = pl.BlockSpec(memory_space=pl.ANY)
 SMEM = pl.BlockSpec(memory_space=pltpu.SMEM)
@@ -127,39 +128,53 @@
                 for copy in copies:
                     act(copy)
 
-    for n in range(slots):
+    for n in reversed(range(slots)):
         each_copy(n, lambda copy: copy.start())
     v[..., HD:] = jnp.ones((*v.shape[:3], HD), v.dtype)
     factor = HD ** (-0.5) * math.log2(math.e)
 
-    def block(n, tile, first, parts, both):
-        half = devices // ROWS
-        keep = devices if both else half
-        shift = 0 if both else tile * half
-        spans = [pl.ds((first + part) * devices + shift, keep) for part in range(parts)]
-        query = q[n, pl.ds(tile * half, half)].reshape(half * tokens, HD)
-        scores = [
+    half = devices // ROWS
+    some = half // PIECES
+
+    def score(n, piece, spans):
+        query = q[n, pl.ds(piece * some, some)].reshape(some * tokens, HD)
+        return [
             lax.dot_general(
                 query,
-                k[n, s].reshape(keep * tokens, HD),
+                k[n, s].reshape(s.size * tokens, HD),
                 (((1,), (1,)), ((), ())),
                 preferred_element_type=jnp.float32,
             )
             for s in spans
         ]
-        largest = functools.reduce(
-            jnp.maximum, [jnp.max(score, axis=1, keepdims=True) for score in scores]
-        )
+
+    def finish(n, piece, spans, scores):
+        lanes = [score[:, i : i + HD] for score in scores for i in range(0, score.shape[1], HD)]
+        largest = jnp.max(functools.reduce(jnp.maximum, lanes), axis=1, keepdims=True)
         mixed = None
         for s, score in zip(spans, scores):
             probs = jnp.exp2((score - largest) * factor).astype(jnp.bfloat16)
-            value = v[n, s].reshape(keep * tokens, 2 * HD)
+            value = v[n, s].reshape(s.size * tokens, 2 * HD)
             term = jnp.dot(probs, value, preferred_element_type=jnp.float32)
             mixed = term if mixed is None else mixed + term
         result = mixed[:, :HD] / mixed[:, HD:]
-        out[pl.ds(tile * half, half), n] = result.astype(out.dtype).reshape(half, tokens, HD)
-
-    def each(n, carry):
+        out[pl.ds(piece * some, some), n] = result.astype(out.dtype).reshape(some, tokens, HD)
+
+    def block(n, pieces, first, parts, both):
+        def spans(piece):
+            keep = devices if both else half
+            shift = 0 if both else piece // PIECES * half
+            return [pl.ds((first + part) * devices + shift, keep) for part in range(parts)]
+
+        ahead = score(n, pieces[0], spans(pieces[0]))
+        for this, after in zip(pieces, [*pieces[1:], None]):
+            now = ahead
+            if after is not None:
+                ahead = score(n, after, spans(after))
+            finish(n, this, spans(this), now)
+
+    def each(step, carry):
+        n = slots - 1 - step
         for i in range(slots):
 
             @pl.when(n == i)
@@ -175,8 +190,13 @@
 
                 @pl.when((parts == number) & ((rows > 0) == both))
                 def _():
+                    if number == 1:
+                        block(n, list(range(ROWS * PIECES)), first, number, both)
+                        return
+
                     def tiles(tile, inner):
-                        block(n, tile, first, number, both)
+                        pieces = [tile * PIECES + i for i in range(PIECES)]
+                        block(n, pieces, first, number, both)
                         return inner
 
                     lax.fori_loop(0, ROWS, tiles, 0)

time: 98.6 us -> 94.7 us (0.960)
  Pallas kernels: 24.6 us -> 21.5 us
    pallas_call x1, Pallas kernels: 14.6 us -> 11.5 us  [call_attend(): pl.pallas_call(functools.partial(attend, near, slots, len(sides) > 2), ou...]
where the time goes in v3:
time: 94.7 us; the launch traced here: 94.3 us
  waiting for transfers between devices  32.7 us (35%)
  Pallas kernels  21.5 us (23%)
  blocking collectives  21.3 us (22%)
  starting transfers between devices  17.3 us (18%)
    all_to_all x2, waiting for transfers between devices, swap(): lax.all_to_all(array, 'head', split_axis=0, concat_axis=0, tiled=True)  32.7 us
    all_to_all x1, blocking collectives, swap(): lax.all_to_all(array, 'head', split_axis=0, concat_axis=0, tiled=True)  21.3 us
    pallas_call x1, Pallas kernels, call_attend(): pl.pallas_call(functools.partial(attend, near, slots, len(sides) > 2), ou...  11.5 us
    all_to_all x2, starting transfers between devices, swap(): lax.all_to_all(array, 'head', split_axis=0, concat_axis=0, tiled=True)  11.1 us
    pallas_call x1, Pallas kernels, shards(): pl.pallas_call(functools.partial(pack_first, near), out_shape=(packed(blo...  4.07 us
    pallas_call x1, Pallas kernels, shards(): pl.pallas_call(functools.partial(pack_second, tuple(range(slots)), far),...  3.48 us
    ppermute x1, starting transfers between devices, neighbours(): lax.ppermute(array, 'seq', [(i, i + 1) for i in range(ends)])  3.44 us
    ppermute x1, starting transfers between devices, neighbours(): lax.ppermute(array, 'seq', [(i + 1, i) for i in range(ends)])  2.76 us
  transfers between devices with their start and end apart: 4, of which 2 were waited for; matrix products, arithmetic and copies ran while one was open for 1% of the time, Pallas kernels for 4%

profile of v3, /device:TPU:1, one launch (start us, length us, event | category | flops | bytes accessed | tf_op | source)
XLA Modules:
  0.0 94.3 jit_solution(15822544709646350367)
XLA Ops:
  0.0 4.1 %pack_near_keys_values.1 = (bf16[8,6,96,128]{3,2,1,0:T(8,128)(2,1)}, s32[40]{0:T(128)S(1)}) custom-call(s32[3,40]{1,0:T(4,128)} %bitcast.1, bf16[96,5120]{1,0:T(8,128)(2,1)} %keys.3, bf16[96,5120]{1,0:T(8,128)(2,1)} %values.3), custom_call_target="tpu_custom_call" | custom-call | bytes 2359296 | tf_op jit(solution)/shard_map/pack_near_keys_values/pallas_call | solution.py:260
  4.1 7.5 %all-to-all-start.1 = ((bf16[8,6,96,128]{3,2,1,0:T(8,128)(2,1)}), bf16[8,6,96,128]{3,2,1,0:T(8,128)(2,1)S(1)}, u32[]{:S(2)}, u32[]{:S(2)}) async-start(bf16[8,6,96,128]{3,2,1,0:T(8,128)(2,1)} %get-tuple-element.47), calls=%async_computation.1 | async-start | bytes 2359296 | tf_op jit(solution)/shard_map/all_to_all | solution.py:250
  11.6 3.5 %pack_queries_and_rest.1 = bf16[8,9,96,128]{3,2,1,0:T(8,128)(2,1)} custom-call(s32[40]{0:T(128)S(1)} %get-tuple-element.46.order, bf16[96,5120]{1,0:T(8,128)(2,1)} %queries.1, bf16[96,5120]{1,0:T(8,128)(2,1)} %keys.3, bf16[96,5120]{1,0:T(8,128)(2,1)} %values.3), custom_call_target="tpu_custom_call" | custom-call | bytes 3538944 | tf_op jit(solution)/shard_map/pack_queries_and_rest/pallas_call | solution.py:271
  15.1 0.0 copy-start
  15.1 15.2 %all-to-all-done.1 = bf16[8,6,96,128]{3,2,1,0:T(8,128)(2,1)S(1)} async-done(((bf16[8,6,96,128]{3,2,1,0:T(8,128)(2,1)}), bf16[8,6,96,128]{3,2,1,0:T(8,128)(2,1)S(1)}, u32[]{:S(2)}, u32[]{:S(2)}) %all-to-all-start.1) | async-done | bytes 1179680 | tf_op jit(solution)/shard_map/all_to_all | solution.py:250
  30.3 3.6 %all-to-all-start = ((bf16[8,9,96,128]{3,2,1,0:T(8,128)(2,1)}), bf16[8,9,96,128]{3,2,1,0:T(8,128)(2,1)S(1)}, u32[]{:S(2)}, u32[]{:S(2)}) async-start(bf16[8,9,96,128]{3,2,1,0:T(8,128)(2,1)} %pack_queries_and_rest.1), calls=%async_computation | async-start | bytes 3538944 | tf_op jit(solution)/shard_map/all_to_all | solution.py:250
  33.9 2.8 %collective-permute-start.3 = (bf16[8,6,96,128]{3,2,1,0:T(8,128)(2,1)S(1)}, bf16[8,6,96,128]{3,2,1,0:T(8,128)(2,1)}, u32[]{:S(2)}, u32[]{:S(2)}) collective-permute-start(bf16[8,6,96,128]{3,2,1,0:T(8,128)(2,1)S(1)} %all-to-all-done.1), channel_id=1, source_target_pairs={{8,0},{16,8},{24,16},{32,24},{40,32},{48,40},{56,48},{64,56},{72,6... | collective-permute-start | bytes 3538952 | tf_op jit(solution)/shard_map/ppermute | solution.py:256
  36.6 3.4 %collective-permute-start.2 = (bf16[8,6,96,128]{3,2,1,0:T(8,128)(2,1)S(1)}, bf16[8,6,96,128]{3,2,1,0:T(8,128)(2,1)}, u32[]{:S(2)}, u32[]{:S(2)}) collective-permute-start(bf16[8,6,96,128]{3,2,1,0:T(8,128)(2,1)S(1)} %all-to-all-done.1), channel_id=1, source_target_pairs={{0,8},{8,16},{16,24},{24,32},{32,40},{40,48},{48,56},{56,64},{64,7... | collective-permute-start | bytes 3538952 | tf_op jit(solution)/shard_map/ppermute | solution.py:255
  40.1 0.0 copy-done
  40.1 0.6 slice_reduce_fusion
  41.4 17.5 %all-to-all-done = bf16[8,9,96,128]{3,2,1,0:T(8,128)(2,1)S(1)} async-done(((bf16[8,9,96,128]{3,2,1,0:T(8,128)(2,1)}), bf16[8,9,96,128]{3,2,1,0:T(8,128)(2,1)S(1)}, u32[]{:S(2)}, u32[]{:S(2)}) %all-to-all-start) | async-done | bytes 1769504 | tf_op jit(solution)/shard_map/all_to_all | solution.py:250
  58.9 0.0 collective-permute-done.3
  58.9 0.0 collective-permute-done.2
  58.9 11.8 %conditional.1 = (bf16[8,5,96,128]{3,2,1,0:T(8,128)(2,1)}) conditional(s32[]{:T(128)} %convert_element_type.3, (s32[40]{0:T(128)S(1)}, s32[3,40]{1,0:T(4,128)S(1)}, bf16[8,9,96,128]{3,2,1,0:T(8,128)(2,1)S(1)}, bf16[8,6,96,128]{3,2,1,0:T(8,128)(2,1)S(1)}, bf16[8,6,96,128]{3,2,1,0:T(8,128)(2,1)}, ...), branch_computations={%region_1.0_spmd, %region_2.0_spmd} | conditional | flops 3019898880 | bytes 15728728 | solution.py:294
  58.9 11.5 %attend_near_slots_wide.1 = bf16[8,5,96,128]{3,2,1,0:T(8,128)(2,1)} custom-call(s32[40]{0:T(128)S(1)} %get-tuple-element.32.order, s32[3,40]{1,0:T(4,128)S(1)} %get-tuple-element.33.windows, bf16[8,9,96,128]{3,2,1,0:T(8,128)(2,1)S(1)} %get-tuple-element.34.rest, bf16[8,6,96,128]{3,2,1,0:T(8,128)(2,1)S(1)} %get-tuple-element.35.near_kv, ...), custom_call_target="tpu_custom_call" | custom-call | flops 3019898880 | bytes 7864320 | tf_op jit(solution)/shard_map/cond/branch_0_fun/attend_near_slots_wide/pallas_call | solution.py:213
  70.6 21.3 %all_to_all.15.blocks = bf16[8,5,96,128]{3,2,1,0:T(8,128)(2,1)} all-to-all(bf16[8,5,96,128]{3,2,1,0:T(8,128)(2,1)} %get-tuple-element.48), channel_id=1, replica_groups=mesh['cfg'=2,'seq'=32,'head'=8] {'head'}, dimensions={0} | all-to-all | bytes 1966080 | tf_op jit(solution)/shard_map/all_to_all | solution.py:250
  91.9 2.4 %unpack_attended.1 = bf16[96,5120]{1,0:T(8,128)(2,1)} custom-call(s32[40]{0:T(128)S(1)} %get-tuple-element.46.order, bf16[8,5,96,128]{3,2,1,0:T(8,128)(2,1)} %all_to_all.15.blocks), custom_call_target="tpu_custom_call" | custom-call | bytes 1966080 | tf_op jit(solution)/shard_map/unpack_attended/pallas_call | solution.py:296
Async XLA Ops:
  4.1 26.2 %all-to-all-start.1 = ((bf16[8,6,96,128]{3,2,1,0:T(8,128)(2,1)}), bf16[8,6,96,128]{3,2,1,0:T(8,128)(2,1)S(1)}, u32[]{:S(2)}, u32[]{:S(2)}) async-start(bf16[8,6,96,128]{3,2,1,0:T(8,128)(2,1)} %get-tuple-element.47), calls=%async_computation.1 | async-start | bytes 2359296 | tf_op jit(solution)/shard_map/all_to_all | solution.py:250
  15.1 25.1 %copy-start = (s32[40,3]{0,1:T(4,128)S(1)}, s32[40,3]{0,1:T(4,128)}, u32[]{:S(2)}) copy-start(s32[40,3]{0,1:T(4,128)} %param.9) | copy-start | bytes 1444
  30.3 28.6 %all-to-all-start = ((bf16[8,9,96,128]{3,2,1,0:T(8,128)(2,1)}), bf16[8,9,96,128]{3,2,1,0:T(8,128)(2,1)S(1)}, u32[]{:S(2)}, u32[]{:S(2)}) async-start(bf16[8,9,96,128]{3,2,1,0:T(8,128)(2,1)} %pack_queries_and_rest.1), calls=%async_computation | async-start | bytes 3538944 | tf_op jit(solution)/shard_map/all_to_all | solution.py:250
  33.9 25.0 %collective-permute-start.3 = (bf16[8,6,96,128]{3,2,1,0:T(8,128)(2,1)S(1)}, bf16[8,6,96,128]{3,2,1,0:T(8,128)(2,1)}, u32[]{:S(2)}, u32[]{:S(2)}) collective-permute-start(bf16[8,6,96,128]{3,2,1,0:T(8,128)(2,1)S(1)} %all-to-all-done.1), channel_id=1, source_target_pairs={{8,0},{16,8},{24,16},{32,24},{40,32},{48,40},{56,48},{64,56},{72,6... | collective-permute-start | bytes 3538952 | tf_op jit(solution)/shard_map/ppermute | solution.py:256
  36.6 22.2 %collective-permute-start.2 = (bf16[8,6,96,128]{3,2,1,0:T(8,128)(2,1)S(1)}, bf16[8,6,96,128]{3,2,1,0:T(8,128)(2,1)}, u32[]{:S(2)}, u32[]{:S(2)}) collective-permute-start(bf16[8,6,96,128]{3,2,1,0:T(8,128)(2,1)S(1)} %all-to-all-done.1), channel_id=1, source_target_pairs={{0,8},{8,16},{16,24},{24,32},{32,40},{40,48},{48,56},{56,64},{64,7... | collective-permute-start | bytes 3538952 | tf_op jit(solution)/shard_map/ppermute | solution.py:255

commit v4 on v3

--- a/solution.py
+++ b/solution.py
@@ -63,7 +63,10 @@
 
 
 def pack_first(near, windows, keys, values, packed, order):
-    sort_heads(windows, order)
+    @pl.when(pl.program_id(0) == 0)
+    def _():
+        sort_heads(windows, order)
+
     pack(order, ((keys, near), (values, near)), packed)
 
 
@@ -71,23 +74,29 @@
     pack(order, ((queries, slots), (keys, far), (values, far)), packed)
 
 
-def unpack(order, blocks, out):
-    devices, slots = blocks.shape[:2]
+def unpack(order, first, second, out):
+    devices = first.shape[0]
     for device in range(devices):
-        for slot in range(slots):
-            head = order[rank_of(device, slot, devices)]
-            out[:, column(head)] = blocks[device, slot]
-
-
-def attend(near, slots, wide, order, windows, rest, near_kv, *refs):
+        at = 0
+        for array in (first, second):
+            for block in range(array.shape[1]):
+                head = order[rank_of(device, at, devices)]
+                out[:, column(head)] = array[device, block]
+                at += 1
+
+
+def attend(slots, at, order, windows, queries, own, *refs):
     *sides, out, q, k, v, sems = refs
-    devices, tokens = q.shape[1:3]
-    far = slots - near
+    q_at, own_at = at
+    has_sides = bool(sides)
+    count, (devices, tokens) = len(slots), q.shape[1:3]
+    mid = 1 if has_sides else 0
     layer, device, layers = lax.axis_index("seq"), lax.axis_index("head"), lax.axis_size("seq")
 
     def extents(n):
-        back = jnp.where(n % 2 == 0, device, devices - 1 - device)
-        head = order[n * devices + back]
+        slot = slots[0] + n
+        back = jnp.where(slot % 2 == 0, device, devices - 1 - device)
+        head = order[slot * devices + back]
         return windows[0, head], windows[1, head]
 
     def pair(n, part, array, k_at, v_at):
@@ -100,22 +109,16 @@
         )
 
     def own_copies(n):
-        query = pltpu.make_async_copy(rest.at[:, n], q.at[n], sems.at[n, 0])
-        if n < near:
-            return (query, *pair(n, 1, near_kv, n, near + n))
-        return (query, *pair(n, 1, rest, slots + n - near, slots + far + n - near))
+        query = pltpu.make_async_copy(queries.at[:, q_at + n], q.at[n], sems.at[n, 0])
+        return (query, *pair(n, mid, own, own_at + n, own_at + count + n))
 
     def side_copies(n):
+        if not has_sides:
+            return ()
         sight, _ = extents(n)
-        if n < near:
-            arrays, k_at, v_at = sides[:2], n, near + n
-        elif wide:
-            arrays, k_at, v_at = sides[2:], n - near, far + n - near
-        else:
-            return ()
         return (
-            ((sight > 0) & (layer > 0), pair(n, 0, arrays[0], k_at, v_at)),
-            ((sight > 0) & (layer < layers - 1), pair(n, 2, arrays[1], k_at, v_at)),
+            ((sight > 0) & (layer > 0), pair(n, 0, sides[0], n, count + n)),
+            ((sight > 0) & (layer < layers - 1), pair(n, 2, sides[1], n, count + n)),
         )
 
     def each_copy(n, act):
@@ -128,7 +131,7 @@
                 for copy in copies:
                     act(copy)
 
-    for n in reversed(range(slots)):
+    for n in reversed(range(count)):
         each_copy(n, lambda copy: copy.start())
     v[..., HD:] = jnp.ones((*v.shape[:3], HD), v.dtype)
     factor = HD ** (-0.5) * math.log2(math.e)
@@ -174,19 +177,21 @@
             finish(n, this, spans(this), now)
 
     def each(step, carry):
-        n = slots - 1 - step
-        for i in range(slots):
+        n = count - 1 - step
+        for i in range(count):
 
             @pl.when(n == i)
             def _():
                 each_copy(i, lambda copy: copy.wait())
 
         sight, rows = extents(n)
-        first = jnp.where((sight > 0) & (layer > 0), 0, 1)
-        last = jnp.where((sight > 0) & (layer < layers - 1), 2, 1)
+        first, last = mid, mid
+        if has_sides:
+            first = jnp.where((sight > 0) & (layer > 0), 0, 1)
+            last = jnp.where((sight > 0) & (layer < layers - 1), 2, 1)
         parts = last - first + 1
         for both in (False, True):
-            for number in (1, 2, 3):
+            for number in (1, 2, 3) if has_sides else (1,):
 
                 @pl.when((parts == number) & ((rows > 0) == both))
                 def _():
@@ -203,30 +208,31 @@
 
         return carry
 
-    lax.fori_loop(0, slots, each, 0)
-
-
-def call_attend(near, slots, order, windows, rest, near_kv, sides, name):
-    devices, _, tokens, _ = rest.shape
-    span = devices * tokens
-    pairs = slots * span * span * 2
+    lax.fori_loop(0, count, each, 0)
+
+
+def call_attend(slots, at, order, windows, queries, own, sides, name):
+    devices, _, tokens, _ = own.shape
+    count, span = len(slots), devices * tokens
+    layers = 3 if sides else 1
+    pairs = count * span * span * layers
     return pl.pallas_call(
-        functools.partial(attend, near, slots, len(sides) > 2),
-        out_shape=jax.ShapeDtypeStruct((devices, slots, tokens, HD), jnp.bfloat16),
+        functools.partial(attend, slots, at),
+        out_shape=jax.ShapeDtypeStruct((devices, count, tokens, HD), jnp.bfloat16),
         in_specs=[SMEM] * 2 + [ANY] * (2 + len(sides)),
         out_specs=VMEM,
         scratch_shapes=[
-            pltpu.VMEM((slots, devices, tokens, HD), jnp.bfloat16),
-            pltpu.VMEM((slots, 3 * devices, tokens, HD), jnp.bfloat16),
-            pltpu.VMEM((slots, 3 * devices, tokens, 2 * HD), jnp.bfloat16),
-            pltpu.SemaphoreType.DMA((slots, 7)),
+            pltpu.VMEM((count, devices, tokens, HD), jnp.bfloat16),
+            pltpu.VMEM((count, layers * devices, tokens, HD), jnp.bfloat16),
+            pltpu.VMEM((count, layers * devices, tokens, 2 * HD), jnp.bfloat16),
+            pltpu.SemaphoreType.DMA((count, 7)),
         ],
         compiler_params=pltpu.CompilerParams(vmem_limit_bytes=48 * 2**20),
         cost_estimate=pl.CostEstimate(
-            flops=4 * pairs * HD, bytes_accessed=16 * slots * span * HD, transcendentals=pairs
+            flops=4 * pairs * HD, bytes_accessed=16 * count * span * HD, transcendentals=pairs
         ),
         name=name,
-    )(order, windows, rest, near_kv, *sides)
+    )(order, windows, queries, own, *sides)
 
 
 def shards(queries, keys, values, windows):
@@ -237,13 +243,19 @@
     slots = heads // devices
     near, far = tuple(range(NEAR)), tuple(range(NEAR, slots))
     windows = windows.T
-
-    def packed(blocks):
-        return jax.ShapeDtypeStruct((devices, blocks, tokens, HD), jnp.bfloat16)
-
-    def moved(blocks):
+    steps = 2 if tokens % 32 == 0 else 1
+    some = tokens // steps
+    rows = pl.BlockSpec((some, model), lambda i: (i, 0))
+
+    def blocks_of(count):
+        return pl.BlockSpec((devices, count, some, HD), lambda i: (0, 0, i, 0))
+
+    def packed(count):
+        return jax.ShapeDtypeStruct((devices, count, tokens, HD), jnp.bfloat16)
+
+    def moved(count):
         return pl.CostEstimate(
-            flops=0, bytes_accessed=4 * devices * blocks * tokens * HD, transcendentals=0
+            flops=0, bytes_accessed=4 * devices * count * tokens * HD, transcendentals=0
         )
 
     def swap(array):
@@ -259,9 +271,10 @@
     blocks = 2 * len(near)
     first, order = pl.pallas_call(
         functools.partial(pack_first, near),
+        grid=(steps,),
         out_shape=(packed(blocks), jax.ShapeDtypeStruct((heads,), jnp.int32)),
-        in_specs=[SMEM, VMEM, VMEM],
-        out_specs=(VMEM, SMEM),
+        in_specs=[SMEM, rows, rows],
+        out_specs=(blocks_of(blocks), SMEM),
         cost_estimate=moved(blocks),
         name="pack_near_keys_values",
     )(windows, keys, values)
@@ -270,37 +283,43 @@
     blocks = slots + 2 * len(far)
     second = pl.pallas_call(
         functools.partial(pack_second, tuple(range(slots)), far),
+        grid=(steps,),
         out_shape=packed(blocks),
-        in_specs=[SMEM, VMEM, VMEM, VMEM],
-        out_specs=VMEM,
+        in_specs=[SMEM, rows, rows, rows],
+        out_specs=blocks_of(blocks),
         cost_estimate=moved(blocks),
         name="pack_queries_and_rest",
     )(order, queries, keys, values)
     sides = neighbours(near_kv)
     rest = swap(second)
 
-    def with_far():
+    def with_sides():
+        far_sides = neighbours(rest[:, slots:])
         return call_attend(
-            NEAR, slots, order, windows, rest, near_kv, (*sides, *neighbours(rest[:, slots:])),
-            "attend_all_slots_wide",
-        )
-
-    def without_far():
+            far, (NEAR, slots), order, windows, rest, rest, far_sides,
+            "attend_far_slots_three_layers",
+        )
+
+    def own_layer():
         return call_attend(
-            NEAR, slots, order, windows, rest, near_kv, sides, "attend_near_slots_wide"
+            far, (NEAR, slots), order, windows, rest, rest, (), "attend_far_slots_own_layer"
         )
 
     wide = jnp.sum(windows[0]) > NEAR * devices
-    attended = swap(lax.cond(wide, with_far, without_far))
+    far_back = swap(lax.cond(wide, with_sides, own_layer))
+    near_back = swap(
+        call_attend(near, (0, 0), order, windows, rest, near_kv, sides, "attend_near_slots")
+    )
 
     return pl.pallas_call(
         unpack,
+        grid=(steps,),
         out_shape=jax.ShapeDtypeStruct((tokens, model), jnp.bfloat16),
-        in_specs=[SMEM, VMEM],
-        out_specs=VMEM,
+        in_specs=[SMEM, blocks_of(len(near)), blocks_of(len(far))],
+        out_specs=rows,
         cost_estimate=moved(slots),
         name="unpack_attended",
-    )(order, attended)
+    )(order, near_back, far_back)
 
 
 def solution(mesh):

time: 94.7 us -> 95.5 us (level); the launches traced: 94.3 us -> 94 us
  blocking collectives: 21.3 us -> 16.1 us
  starting transfers between devices: 17.3 us -> 21.5 us
    all_to_all x1, blocking collectives: 21.3 us -> 16.1 us  [swap(): lax.all_to_all(array, 'head', split_axis=0, concat_axis=0, tiled=True)]
    all_to_all x2 -> x3, starting transfers between devices: 11.1 us -> 15.3 us  [swap(): lax.all_to_all(array, 'head', split_axis=0, concat_axis=0, tiled=True)]
    pallas_call x3 -> x4, Pallas kernels: 18 us -> 18.7 us  [the longest x2 13 us: call_attend(): pl.pallas_call(functools.partial(attend, slots, at), out_shape=jax.ShapeD...]
    all_to_all x2 -> x3, waiting for transfers between devices: 32.7 us -> 33.4 us  [swap(): lax.all_to_all(array, 'head', split_axis=0, concat_axis=0, tiled=True)]
  transfers between devices with their start and end apart: 4 -> 5, of which waited for: 2 -> 3; matrix products, arithmetic and copies ran while one was open for 1% -> 1% of each run, Pallas kernels for 4% -> 17%
where the time goes in v4:
time: 95.5 us; the launch traced here: 94 us
  waiting for transfers between devices  33.4 us (35%)
  Pallas kernels  21.7 us (23%)
  starting transfers between devices  21.5 us (23%)
  blocking collectives  16.1 us (17%)
    all_to_all x3, waiting for transfers between devices, swap(): lax.all_to_all(array, 'head', split_axis=0, concat_axis=0, tiled=True)  33.4 us
    all_to_all x1, blocking collectives, swap(): lax.all_to_all(array, 'head', split_axis=0, concat_axis=0, tiled=True)  16.1 us
    all_to_all x3, starting transfers between devices, swap(): lax.all_to_all(array, 'head', split_axis=0, concat_axis=0, tiled=True)  15.3 us
    pallas_call x2, Pallas kernels, call_attend(): pl.pallas_call(functools.partial(attend, slots, at), out_shape=jax.ShapeD...  13 us
    ppermute x1, starting transfers between devices, neighbours(): lax.ppermute(array, 'seq', [(i, i + 1) for i in range(ends)])  4.29 us
    pallas_call x1, Pallas kernels, shards(): pl.pallas_call(functools.partial(pack_first, near), grid=(steps,), out_sh...  3.62 us
    pallas_call x1, Pallas kernels, shards(): pl.pallas_call(functools.partial(pack_second, tuple(range(slots)), far),...  3 us
    pallas_call x1, Pallas kernels, shards(): pl.pallas_call(unpack, grid=(steps,), out_shape=jax.ShapeDtypeStruct((tok...  2.1 us
  transfers between devices with their start and end apart: 5, of which 3 were waited for; matrix products, arithmetic and copies ran while one was open for 1% of the time, Pallas kernels for 17%

profile of v4, /device:TPU:1, one launch (start us, length us, event | category | flops | bytes accessed | tf_op | source)
XLA Modules:
  0.0 94.0 jit_solution(13000202039679580581)
XLA Ops:
  0.0 3.6 %pack_near_keys_values.1 = (bf16[8,6,96,128]{3,2,1,0:T(8,128)(2,1)}, s32[40]{0:T(128)S(1)}) custom-call(s32[3,40]{1,0:T(4,128)} %bitcast.1, bf16[96,5120]{1,0:T(8,128)(2,1)} %keys.3, bf16[96,5120]{1,0:T(8,128)(2,1)} %values.3), custom_call_target="tpu_custom_call" | custom-call | bytes 2359296 | tf_op jit(solution)/shard_map/pack_near_keys_values/pallas_call | solution.py:272
  3.6 7.5 %all-to-all-start.1 = ((bf16[8,6,96,128]{3,2,1,0:T(8,128)(2,1)}), bf16[8,6,96,128]{3,2,1,0:T(8,128)(2,1)S(1)}, u32[]{:S(2)}, u32[]{:S(2)}) async-start(bf16[8,6,96,128]{3,2,1,0:T(8,128)(2,1)} %get-tuple-element.29), calls=%async_computation.1 | async-start | bytes 2359296 | tf_op jit(solution)/shard_map/all_to_all | solution.py:262
  11.1 3.0 %pack_queries_and_rest.1 = bf16[8,9,96,128]{3,2,1,0:T(8,128)(2,1)} custom-call(s32[40]{0:T(128)S(1)} %get-tuple-element.28.order, bf16[96,5120]{1,0:T(8,128)(2,1)} %queries.1, bf16[96,5120]{1,0:T(8,128)(2,1)} %keys.3, bf16[96,5120]{1,0:T(8,128)(2,1)} %values.3), custom_call_target="tpu_custom_call" | custom-call | bytes 3538944 | tf_op jit(solution)/shard_map/pack_queries_and_rest/pallas_call | solution.py:284
  14.1 0.0 copy-start.1
  14.1 15.7 %all-to-all-done.1.own = bf16[8,6,96,128]{3,2,1,0:T(8,128)(2,1)S(1)} async-done(((bf16[8,6,96,128]{3,2,1,0:T(8,128)(2,1)}), bf16[8,6,96,128]{3,2,1,0:T(8,128)(2,1)S(1)}, u32[]{:S(2)}, u32[]{:S(2)}) %all-to-all-start.1) | async-done | bytes 1179680 | tf_op jit(solution)/shard_map/all_to_all | solution.py:262
  29.8 4.3 %all-to-all-start = ((bf16[8,9,96,128]{3,2,1,0:T(8,128)(2,1)}), bf16[8,9,96,128]{3,2,1,0:T(8,128)(2,1)}, u32[]{:S(2)}, u32[]{:S(2)}) async-start(bf16[8,9,96,128]{3,2,1,0:T(8,128)(2,1)} %pack_queries_and_rest.1), calls=%async_computation | async-start | bytes 3538944 | tf_op jit(solution)/shard_map/all_to_all | solution.py:262
  34.1 4.3 %collective-permute-start.2 = (bf16[8,6,96,128]{3,2,1,0:T(8,128)(2,1)S(1)}, bf16[8,6,96,128]{3,2,1,0:T(8,128)(2,1)S(1)}, u32[]{:S(2)}, u32[]{:S(2)}) collective-permute-start(bf16[8,6,96,128]{3,2,1,0:T(8,128)(2,1)S(1)} %all-to-all-done.1.own), channel_id=1, source_target_pairs={{0,8},{8,16},{16,24},{24,32},{32,40},{40,48},{48,56},{56,64},{64,7... | collective-permute-start | bytes 3538952 | tf_op jit(solution)/shard_map/ppermute | solution.py:267
  38.4 1.9 %collective-permute-start.3 = (bf16[8,6,96,128]{3,2,1,0:T(8,128)(2,1)S(1)}, bf16[8,6,96,128]{3,2,1,0:T(8,128)(2,1)}, u32[]{:S(2)}, u32[]{:S(2)}) collective-permute-start(bf16[8,6,96,128]{3,2,1,0:T(8,128)(2,1)S(1)} %all-to-all-done.1.own), channel_id=1, source_target_pairs={{8,0},{16,8},{24,16},{32,24},{40,32},{48,40},{56,48},{64,56},{72,6... | collective-permute-start | bytes 3538952 | tf_op jit(solution)/shard_map/ppermute | solution.py:268
  40.4 0.0 copy-done.1
  40.4 0.6 slice_reduce_fusion
  41.7 17.6 %all-to-all-done.queries = bf16[8,9,96,128]{3,2,1,0:T(8,128)(2,1)} async-done(((bf16[8,9,96,128]{3,2,1,0:T(8,128)(2,1)}), bf16[8,9,96,128]{3,2,1,0:T(8,128)(2,1)}, u32[]{:S(2)}, u32[]{:S(2)}) %all-to-all-start) | async-done | bytes 1769504 | tf_op jit(solution)/shard_map/all_to_all | solution.py:262
  59.2 4.3 %conditional.1 = (bf16[8,2,96,128]{3,2,1,0:T(8,128)(2,1)}) conditional(s32[]{:T(128)} %convert_element_type.3, (s32[40]{0:T(128)S(1)}, s32[3,40]{1,0:T(4,128)S(1)}, bf16[8,9,96,128]{3,2,1,0:T(8,128)(2,1)}) %tuple.15, (bf16[8,9,96,128]{3,2,1,0:T(8,128)(2,1)}, s32[40]{0:T(128)S(1)}, s32[3,40]{1,0:T(4,128)S(1)}) %tuple.16), branch_computations={%region_1.0_spmd, %region_2.0_spmd} | conditional | flops 1811939328 | bytes 11010136 | solution.py:309
  59.2 4.3 %attend_far_slots_own_layer.1 = bf16[8,2,96,128]{3,2,1,0:T(8,128)(2,1)} custom-call(s32[40]{0:T(128)S(1)} %get-tuple-element.20.order, s32[3,40]{1,0:T(4,128)S(1)} %get-tuple-element.21.windows, bf16[8,9,96,128]{3,2,1,0:T(8,128)(2,1)} %get-tuple-element.22.queries.own, bf16[8,9,96,128]{3,2,1,0:T(8,128)(2,1)} %get-tuple-element.22.queries.own), custom_call_target="tpu_custom_call" | custom-call | flops 603979776 | bytes 3145728 | tf_op jit(solution)/shard_map/cond/branch_0_fun/attend_far_slots_own_layer/pallas_call | solution.py:219
  63.6 3.5 %all-to-all-start.3 = ((bf16[8,2,96,128]{3,2,1,0:T(8,128)(2,1)}), bf16[8,2,96,128]{3,2,1,0:T(8,128)(2,1)S(1)}, u32[]{:S(2)}, u32[]{:S(2)}) async-start(bf16[8,2,96,128]{3,2,1,0:T(8,128)(2,1)} %get-tuple-element.30), calls=%async_computation.3 | async-start | bytes 786432 | tf_op jit(solution)/shard_map/all_to_all | solution.py:262
  67.0 0.0 collective-permute-done.2.refs_0_
  67.0 0.0 collective-permute-done.3.refs_1_
  67.1 8.6 %attend_near_slots.1 = bf16[8,3,96,128]{3,2,1,0:T(8,128)(2,1)S(1)} custom-call(s32[40]{0:T(128)S(1)} %get-tuple-element.28.order, s32[3,40]{1,0:T(4,128)S(1)} %bitcast.5, bf16[8,9,96,128]{3,2,1,0:T(8,128)(2,1)} %all-to-all-done.queries, bf16[8,6,96,128]{3,2,1,0:T(8,128)(2,1)S(1)} %all-to-all-done.1.own, ...), custom_call_target="tpu_custom_call" | custom-call | flops 2717908992 | bytes 4718592 | tf_op jit(solution)/shard_map/attend_near_slots/pallas_call | solution.py:219
  75.7 0.1 all-to-all-done.3.second
  75.8 0.0 copy-start
  75.8 16.1 %all_to_all.20.first = bf16[8,3,96,128]{3,2,1,0:T(8,128)(2,1)} all-to-all(bf16[8,3,96,128]{3,2,1,0:T(8,128)(2,1)S(1)} %attend_near_slots.1), channel_id=1, replica_groups=mesh['cfg'=2,'seq'=32,'head'=8] {'head'}, dimensions={0} | all-to-all | bytes 1179648 | tf_op jit(solution)/shard_map/all_to_all | solution.py:262
  91.9 0.0 copy-done
  91.9 2.1 %unpack_attended.1 = bf16[96,5120]{1,0:T(8,128)(2,1)} custom-call(s32[40]{0:T(128)S(1)} %get-tuple-element.28.order, bf16[8,3,96,128]{3,2,1,0:T(8,128)(2,1)} %all_to_all.20.first, bf16[8,2,96,128]{3,2,1,0:T(8,128)(2,1)} %copy-done), custom_call_target="tpu_custom_call" | custom-call | bytes 1966080 | tf_op jit(solution)/shard_map/unpack_attended/pallas_call | solution.py:314
Async XLA Ops:
  3.6 26.2 %all-to-all-start.1 = ((bf16[8,6,96,128]{3,2,1,0:T(8,128)(2,1)}), bf16[8,6,96,128]{3,2,1,0:T(8,128)(2,1)S(1)}, u32[]{:S(2)}, u32[]{:S(2)}) async-start(bf16[8,6,96,128]{3,2,1,0:T(8,128)(2,1)} %get-tuple-element.29), calls=%async_computation.1 | async-start | bytes 2359296 | tf_op jit(solution)/shard_map/all_to_all | solution.py:262
  14.1 26.3 %copy-start.1 = (s32[40,3]{0,1:T(4,128)S(1)}, s32[40,3]{0,1:T(4,128)}, u32[]{:S(2)}) copy-start(s32[40,3]{0,1:T(4,128)} %param.9) | copy-start | bytes 1444
  29.8 29.4 %all-to-all-start = ((bf16[8,9,96,128]{3,2,1,0:T(8,128)(2,1)}), bf16[8,9,96,128]{3,2,1,0:T(8,128)(2,1)}, u32[]{:S(2)}, u32[]{:S(2)}) async-start(bf16[8,9,96,128]{3,2,1,0:T(8,128)(2,1)} %pack_queries_and_rest.1), calls=%async_computation | async-start | bytes 3538944 | tf_op jit(solution)/shard_map/all_to_all | solution.py:262
  34.1 32.9 %collective-permute-start.2 = (bf16[8,6,96,128]{3,2,1,0:T(8,128)(2,1)S(1)}, bf16[8,6,96,128]{3,2,1,0:T(8,128)(2,1)S(1)}, u32[]{:S(2)}, u32[]{:S(2)}) collective-permute-start(bf16[8,6,96,128]{3,2,1,0:T(8,128)(2,1)S(1)} %all-to-all-done.1.own), channel_id=1, source_target_pairs={{0,8},{8,16},{16,24},{24,32},{32,40},{40,48},{48,56},{56,64},{64,7... | collective-permute-start | bytes 3538952 | tf_op jit(solution)/shard_map/ppermute | solution.py:267
  38.4 28.6 %collective-permute-start.3 = (bf16[8,6,96,128]{3,2,1,0:T(8,128)(2,1)S(1)}, bf16[8,6,96,128]{3,2,1,0:T(8,128)(2,1)}, u32[]{:S(2)}, u32[]{:S(2)}) collective-permute-start(bf16[8,6,96,128]{3,2,1,0:T(8,128)(2,1)S(1)} %all-to-all-done.1.own), channel_id=1, source_target_pairs={{8,0},{16,8},{24,16},{32,24},{40,32},{48,40},{56,48},{64,56},{72,6... | collective-permute-start | bytes 3538952 | tf_op jit(solution)/shard_map/ppermute | solution.py:268
  63.6 12.2 %all-to-all-start.3 = ((bf16[8,2,96,128]{3,2,1,0:T(8,128)(2,1)}), bf16[8,2,96,128]{3,2,1,0:T(8,128)(2,1)S(1)}, u32[]{:S(2)}, u32[]{:S(2)}) async-start(bf16[8,2,96,128]{3,2,1,0:T(8,128)(2,1)} %get-tuple-element.30), calls=%async_computation.3 | async-start | bytes 786432 | tf_op jit(solution)/shard_map/all_to_all | solution.py:262
  75.8 16.1 %copy-start = (bf16[8,2,96,128]{3,2,1,0:T(8,128)(2,1)}, bf16[8,2,96,128]{3,2,1,0:T(8,128)(2,1)S(1)}, u32[]{:S(2)}) copy-start(bf16[8,2,96,128]{3,2,1,0:T(8,128)(2,1)S(1)} %all-to-all-done.3.second) | copy-start | bytes 1179652

commit v5 on v3

--- a/solution.py
+++ b/solution.py
@@ -63,7 +63,10 @@
 
 
 def pack_first(near, windows, keys, values, packed, order):
-    sort_heads(windows, order)
+    @pl.when(pl.program_id(0) == 0)
+    def _():
+        sort_heads(windows, order)
+
     pack(order, ((keys, near), (values, near)), packed)
 
 
@@ -237,6 +240,12 @@
     slots = heads // devices
     near, far = tuple(range(NEAR)), tuple(range(NEAR, slots))
     windows = windows.T
+    steps = 2 if tokens % 32 == 0 else 1
+    some = tokens // steps
+    rows = pl.BlockSpec((some, model), lambda i: (i, 0))
+
+    def blocks_of(count):
+        return pl.BlockSpec((devices, count, some, HD), lambda i: (0, 0, i, 0))
 
     def packed(blocks):
         return jax.ShapeDtypeStruct((devices, blocks, tokens, HD), jnp.bfloat16)
@@ -259,9 +268,10 @@
     blocks = 2 * len(near)
     first, order = pl.pallas_call(
         functools.partial(pack_first, near),
+        grid=(steps,),
         out_shape=(packed(blocks), jax.ShapeDtypeStruct((heads,), jnp.int32)),
-        in_specs=[SMEM, VMEM, VMEM],
-        out_specs=(VMEM, SMEM),
+        in_specs=[SMEM, rows, rows],
+        out_specs=(blocks_of(blocks), SMEM),
         cost_estimate=moved(blocks),
         name="pack_near_keys_values",
     )(windows, keys, values)
@@ -270,9 +280,10 @@
     blocks = slots + 2 * len(far)
     second = pl.pallas_call(
         functools.partial(pack_second, tuple(range(slots)), far),
+        grid=(steps,),
         out_shape=packed(blocks),
-        in_specs=[SMEM, VMEM, VMEM, VMEM],
-        out_specs=VMEM,
+        in_specs=[SMEM, rows, rows, rows],
+        out_specs=blocks_of(blocks),
         cost_estimate=moved(blocks),
         name="pack_queries_and_rest",
     )(order, queries, keys, values)
@@ -295,9 +306,10 @@
 
     return pl.pallas_call(
         unpack,
+        grid=(steps,),
         out_shape=jax.ShapeDtypeStruct((tokens, model), jnp.bfloat16),
-        in_specs=[SMEM, VMEM],
-        out_specs=VMEM,
+        in_specs=[SMEM, blocks_of(slots)],
+        out_specs=rows,
         cost_estimate=moved(slots),
         name="unpack_attended",
     )(order, attended)

time: 94.7 us -> 93.9 us (level)
  Pallas kernels: 21.5 us -> 20.2 us
  transfers between devices with their start and end apart: 4 -> 4, of which waited for: 2 -> 2; matrix products, arithmetic and copies ran while one was open for 1% -> 1% of each run, Pallas kernels for 4% -> 3%
where the time goes in v5:
time: 93.9 us; the launch traced here: 93.5 us
  waiting for transfers between devices  33.2 us (35%)
  blocking collectives  21.2 us (23%)
  Pallas kernels  20.2 us (22%)
  starting transfers between devices  17.3 us (18%)
    all_to_all x2, waiting for transfers between devices, swap(): lax.all_to_all(array, 'head', split_axis=0, concat_axis=0, tiled=True)  33.2 us
    all_to_all x1, blocking collectives, swap(): lax.all_to_all(array, 'head', split_axis=0, concat_axis=0, tiled=True)  21.2 us
    pallas_call x1, Pallas kernels, call_attend(): pl.pallas_call(functools.partial(attend, near, slots, len(sides) > 2), ou...  11.5 us
    all_to_all x2, starting transfers between devices, swap(): lax.all_to_all(array, 'head', split_axis=0, concat_axis=0, tiled=True)  11.1 us
    pallas_call x1, Pallas kernels, shards(): pl.pallas_call(functools.partial(pack_first, near), grid=(steps,), out_sh...  3.63 us
    ppermute x1, starting transfers between devices, neighbours(): lax.ppermute(array, 'seq', [(i, i + 1) for i in range(ends)])  3.44 us
    pallas_call x1, Pallas kernels, shards(): pl.pallas_call(functools.partial(pack_second, tuple(range(slots)), far),...  2.96 us
    ppermute x1, starting transfers between devices, neighbours(): lax.ppermute(array, 'seq', [(i + 1, i) for i in range(ends)])  2.76 us
  transfers between devices with their start and end apart: 4, of which 2 were waited for; matrix products, arithmetic and copies ran while one was open for 1% of the time, Pallas kernels for 3%

profile of v5, /device:TPU:1, one launch (start us, length us, event | category | flops | bytes accessed | tf_op | source)
XLA Modules:
  0.0 93.5 jit_solution(8832983032841621443)
XLA Ops:
  0.0 3.6 %pack_near_keys_values.1 = (bf16[8,6,96,128]{3,2,1,0:T(8,128)(2,1)}, s32[40]{0:T(128)S(1)}) custom-call(s32[3,40]{1,0:T(4,128)} %bitcast.1, bf16[96,5120]{1,0:T(8,128)(2,1)} %keys.3, bf16[96,5120]{1,0:T(8,128)(2,1)} %values.3), custom_call_target="tpu_custom_call" | custom-call | bytes 2359296 | tf_op jit(solution)/shard_map/pack_near_keys_values/pallas_call | solution.py:269
  3.6 7.5 %all-to-all-start.1 = ((bf16[8,6,96,128]{3,2,1,0:T(8,128)(2,1)}), bf16[8,6,96,128]{3,2,1,0:T(8,128)(2,1)S(1)}, u32[]{:S(2)}, u32[]{:S(2)}) async-start(bf16[8,6,96,128]{3,2,1,0:T(8,128)(2,1)} %get-tuple-element.47), calls=%async_computation.1 | async-start | bytes 2359296 | tf_op jit(solution)/shard_map/all_to_all | solution.py:259
  11.1 3.0 %pack_queries_and_rest.1 = bf16[8,9,96,128]{3,2,1,0:T(8,128)(2,1)} custom-call(s32[40]{0:T(128)S(1)} %get-tuple-element.46.order, bf16[96,5120]{1,0:T(8,128)(2,1)} %queries.1, bf16[96,5120]{1,0:T(8,128)(2,1)} %keys.3, bf16[96,5120]{1,0:T(8,128)(2,1)} %values.3), custom_call_target="tpu_custom_call" | custom-call | bytes 3538944 | tf_op jit(solution)/shard_map/pack_queries_and_rest/pallas_call | solution.py:281
  14.1 0.0 copy-start
  14.1 15.7 %all-to-all-done.1 = bf16[8,6,96,128]{3,2,1,0:T(8,128)(2,1)S(1)} async-done(((bf16[8,6,96,128]{3,2,1,0:T(8,128)(2,1)}), bf16[8,6,96,128]{3,2,1,0:T(8,128)(2,1)S(1)}, u32[]{:S(2)}, u32[]{:S(2)}) %all-to-all-start.1) | async-done | bytes 1179680 | tf_op jit(solution)/shard_map/all_to_all | solution.py:259
  29.8 3.6 %all-to-all-start = ((bf16[8,9,96,128]{3,2,1,0:T(8,128)(2,1)}), bf16[8,9,96,128]{3,2,1,0:T(8,128)(2,1)S(1)}, u32[]{:S(2)}, u32[]{:S(2)}) async-start(bf16[8,9,96,128]{3,2,1,0:T(8,128)(2,1)} %pack_queries_and_rest.1), calls=%async_computation | async-start | bytes 3538944 | tf_op jit(solution)/shard_map/all_to_all | solution.py:259
  33.4 2.8 %collective-permute-start.3 = (bf16[8,6,96,128]{3,2,1,0:T(8,128)(2,1)S(1)}, bf16[8,6,96,128]{3,2,1,0:T(8,128)(2,1)}, u32[]{:S(2)}, u32[]{:S(2)}) collective-permute-start(bf16[8,6,96,128]{3,2,1,0:T(8,128)(2,1)S(1)} %all-to-all-done.1), channel_id=1, source_target_pairs={{8,0},{16,8},{24,16},{32,24},{40,32},{48,40},{56,48},{64,56},{72,6... | collective-permute-start | bytes 3538952 | tf_op jit(solution)/shard_map/ppermute | solution.py:265
  36.2 3.4 %collective-permute-start.2 = (bf16[8,6,96,128]{3,2,1,0:T(8,128)(2,1)S(1)}, bf16[8,6,96,128]{3,2,1,0:T(8,128)(2,1)}, u32[]{:S(2)}, u32[]{:S(2)}) collective-permute-start(bf16[8,6,96,128]{3,2,1,0:T(8,128)(2,1)S(1)} %all-to-all-done.1), channel_id=1, source_target_pairs={{0,8},{8,16},{16,24},{24,32},{32,40},{40,48},{48,56},{56,64},{64,7... | collective-permute-start | bytes 3538952 | tf_op jit(solution)/shard_map/ppermute | solution.py:264
  39.6 0.0 copy-done
  39.6 0.6 slice_reduce_fusion
  40.9 17.5 %all-to-all-done = bf16[8,9,96,128]{3,2,1,0:T(8,128)(2,1)S(1)} async-done(((bf16[8,9,96,128]{3,2,1,0:T(8,128)(2,1)}), bf16[8,9,96,128]{3,2,1,0:T(8,128)(2,1)S(1)}, u32[]{:S(2)}, u32[]{:S(2)}) %all-to-all-start) | async-done | bytes 1769504 | tf_op jit(solution)/shard_map/all_to_all | solution.py:259
  58.4 0.0 collective-permute-done.3
  58.4 0.0 collective-permute-done.2
  58.4 11.8 %conditional.1 = (bf16[8,5,96,128]{3,2,1,0:T(8,128)(2,1)}) conditional(s32[]{:T(128)} %convert_element_type.3, (s32[40]{0:T(128)S(1)}, s32[3,40]{1,0:T(4,128)S(1)}, bf16[8,9,96,128]{3,2,1,0:T(8,128)(2,1)S(1)}, bf16[8,6,96,128]{3,2,1,0:T(8,128)(2,1)S(1)}, bf16[8,6,96,128]{3,2,1,0:T(8,128)(2,1)}, ...), branch_computations={%region_1.0_spmd, %region_2.0_spmd} | conditional | flops 3019898880 | bytes 15728728 | solution.py:305
  58.4 11.5 %attend_near_slots_wide.1 = bf16[8,5,96,128]{3,2,1,0:T(8,128)(2,1)} custom-call(s32[40]{0:T(128)S(1)} %get-tuple-element.32.order, s32[3,40]{1,0:T(4,128)S(1)} %get-tuple-element.33.windows, bf16[8,9,96,128]{3,2,1,0:T(8,128)(2,1)S(1)} %get-tuple-element.34.rest, bf16[8,6,96,128]{3,2,1,0:T(8,128)(2,1)S(1)} %get-tuple-element.35.near_kv, ...), custom_call_target="tpu_custom_call" | custom-call | flops 3019898880 | bytes 7864320 | tf_op jit(solution)/shard_map/cond/branch_0_fun/attend_near_slots_wide/pallas_call | solution.py:216
  70.2 21.2 %all_to_all.15.blocks = bf16[8,5,96,128]{3,2,1,0:T(8,128)(2,1)} all-to-all(bf16[8,5,96,128]{3,2,1,0:T(8,128)(2,1)} %get-tuple-element.48), channel_id=1, replica_groups=mesh['cfg'=2,'seq'=32,'head'=8] {'head'}, dimensions={0} | all-to-all | bytes 1966080 | tf_op jit(solution)/shard_map/all_to_all | solution.py:259
  91.4 2.1 %unpack_attended.1 = bf16[96,5120]{1,0:T(8,128)(2,1)} custom-call(s32[40]{0:T(128)S(1)} %get-tuple-element.46.order, bf16[8,5,96,128]{3,2,1,0:T(8,128)(2,1)} %all_to_all.15.blocks), custom_call_target="tpu_custom_call" | custom-call | bytes 1966080 | tf_op jit(solution)/shard_map/unpack_attended/pallas_call | solution.py:307
Async XLA Ops:
  3.6 26.2 %all-to-all-start.1 = ((bf16[8,6,96,128]{3,2,1,0:T(8,128)(2,1)}), bf16[8,6,96,128]{3,2,1,0:T(8,128)(2,1)S(1)}, u32[]{:S(2)}, u32[]{:S(2)}) async-start(bf16[8,6,96,128]{3,2,1,0:T(8,128)(2,1)} %get-tuple-element.47), calls=%async_computation.1 | async-start | bytes 2359296 | tf_op jit(solution)/shard_map/all_to_all | solution.py:259
  14.1 25.6 %copy-start = (s32[40,3]{0,1:T(4,128)S(1)}, s32[40,3]{0,1:T(4,128)}, u32[]{:S(2)}) copy-start(s32[40,3]{0,1:T(4,128)} %param.9) | copy-start | bytes 1444
  29.8 28.6 %all-to-all-start = ((bf16[8,9,96,128]{3,2,1,0:T(8,128)(2,1)}), bf16[8,9,96,128]{3,2,1,0:T(8,128)(2,1)S(1)}, u32[]{:S(2)}, u32[]{:S(2)}) async-start(bf16[8,9,96,128]{3,2,1,0:T(8,128)(2,1)} %pack_queries_and_rest.1), calls=%async_computation | async-start | bytes 3538944 | tf_op jit(solution)/shard_map/all_to_all | solution.py:259
  33.4 25.0 %collective-permute-start.3 = (bf16[8,6,96,128]{3,2,1,0:T(8,128)(2,1)S(1)}, bf16[8,6,96,128]{3,2,1,0:T(8,128)(2,1)}, u32[]{:S(2)}, u32[]{:S(2)}) collective-permute-start(bf16[8,6,96,128]{3,2,1,0:T(8,128)(2,1)S(1)} %all-to-all-done.1), channel_id=1, source_target_pairs={{8,0},{16,8},{24,16},{32,24},{40,32},{48,40},{56,48},{64,56},{72,6... | collective-permute-start | bytes 3538952 | tf_op jit(solution)/shard_map/ppermute | solution.py:265
  36.2 22.2 %collective-permute-start.2 = (bf16[8,6,96,128]{3,2,1,0:T(8,128)(2,1)S(1)}, bf16[8,6,96,128]{3,2,1,0:T(8,128)(2,1)}, u32[]{:S(2)}, u32[]{:S(2)}) collective-permute-start(bf16[8,6,96,128]{3,2,1,0:T(8,128)(2,1)S(1)} %all-to-all-done.1), channel_id=1, source_target_pairs={{0,8},{8,16},{16,24},{24,32},{32,40},{40,48},{48,56},{56,64},{64,7... | collective-permute-start | bytes 3538952 | tf_op jit(solution)/shard_map/ppermute | solution.py:264

commit v6 on v5

--- a/solution.py
+++ b/solution.py
@@ -193,7 +193,7 @@
 
                 @pl.when((parts == number) & ((rows > 0) == both))
                 def _():
-                    if number == 1:
+                    if number == 1 or not both:
                         block(n, list(range(ROWS * PIECES)), first, number, both)
                         return
 

time: 93.9 us -> 93.6 us (level)
  no operation moved by 1% of the time
where the time goes in v6:
time: 93.6 us; the launch traced here: 92.9 us
  waiting for transfers between devices  33.2 us (35%)
  blocking collectives  21.2 us (23%)
  Pallas kernels  19.7 us (21%)
  starting transfers between devices  17.3 us (18%)
    all_to_all x2, waiting for transfers between devices, swap(): lax.all_to_all(array, 'head', split_axis=0, concat_axis=0, tiled=True)  33.2 us
    all_to_all x1, blocking collectives, swap(): lax.all_to_all(array, 'head', split_axis=0, concat_axis=0, tiled=True)  21.2 us
    all_to_all x2, starting transfers between devices, swap(): lax.all_to_all(array, 'head', split_axis=0, concat_axis=0, tiled=True)  11.1 us
    pallas_call x1, Pallas kernels, call_attend(): pl.pallas_call(functools.partial(attend, near, slots, len(sides) > 2), ou...  11 us
    pallas_call x1, Pallas kernels, shards(): pl.pallas_call(functools.partial(pack_first, near), grid=(steps,), out_sh...  3.63 us
    ppermute x1, starting transfers between devices, neighbours(): lax.ppermute(array, 'seq', [(i, i + 1) for i in range(ends)])  3.44 us
    pallas_call x1, Pallas kernels, shards(): pl.pallas_call(functools.partial(pack_second, tuple(range(slots)), far),...  2.96 us
    ppermute x1, starting transfers between devices, neighbours(): lax.ppermute(array, 'seq', [(i + 1, i) for i in range(ends)])  2.76 us
  transfers between devices with their start and end apart: 4, of which 2 were waited for; matrix products, arithmetic and copies ran while one was open for 1% of the time, Pallas kernels for 3%

profile of v6, /device:TPU:1, one launch (start us, length us, event | category | flops | bytes accessed | tf_op | source)
XLA Modules:
  0.0 92.9 jit_solution(15550256671580008568)
XLA Ops:
  0.0 3.6 %pack_near_keys_values.1 = (bf16[8,6,96,128]{3,2,1,0:T(8,128)(2,1)}, s32[40]{0:T(128)S(1)}) custom-call(s32[3,40]{1,0:T(4,128)} %bitcast.1, bf16[96,5120]{1,0:T(8,128)(2,1)} %keys.3, bf16[96,5120]{1,0:T(8,128)(2,1)} %values.3), custom_call_target="tpu_custom_call" | custom-call | bytes 2359296 | tf_op jit(solution)/shard_map/pack_near_keys_values/pallas_call | solution.py:269
  3.6 7.5 %all-to-all-start.1 = ((bf16[8,6,96,128]{3,2,1,0:T(8,128)(2,1)}), bf16[8,6,96,128]{3,2,1,0:T(8,128)(2,1)S(1)}, u32[]{:S(2)}, u32[]{:S(2)}) async-start(bf16[8,6,96,128]{3,2,1,0:T(8,128)(2,1)} %get-tuple-element.47), calls=%async_computation.1 | async-start | bytes 2359296 | tf_op jit(solution)/shard_map/all_to_all | solution.py:259
  11.1 3.0 %pack_queries_and_rest.1 = bf16[8,9,96,128]{3,2,1,0:T(8,128)(2,1)} custom-call(s32[40]{0:T(128)S(1)} %get-tuple-element.46.order, bf16[96,5120]{1,0:T(8,128)(2,1)} %queries.1, bf16[96,5120]{1,0:T(8,128)(2,1)} %keys.3, bf16[96,5120]{1,0:T(8,128)(2,1)} %values.3), custom_call_target="tpu_custom_call" | custom-call | bytes 3538944 | tf_op jit(solution)/shard_map/pack_queries_and_rest/pallas_call | solution.py:281
  14.1 0.0 copy-start
  14.1 15.7 %all-to-all-done.1 = bf16[8,6,96,128]{3,2,1,0:T(8,128)(2,1)S(1)} async-done(((bf16[8,6,96,128]{3,2,1,0:T(8,128)(2,1)}), bf16[8,6,96,128]{3,2,1,0:T(8,128)(2,1)S(1)}, u32[]{:S(2)}, u32[]{:S(2)}) %all-to-all-start.1) | async-done | bytes 1179680 | tf_op jit(solution)/shard_map/all_to_all | solution.py:259
  29.8 3.6 %all-to-all-start = ((bf16[8,9,96,128]{3,2,1,0:T(8,128)(2,1)}), bf16[8,9,96,128]{3,2,1,0:T(8,128)(2,1)S(1)}, u32[]{:S(2)}, u32[]{:S(2)}) async-start(bf16[8,9,96,128]{3,2,1,0:T(8,128)(2,1)} %pack_queries_and_rest.1), calls=%async_computation | async-start | bytes 3538944 | tf_op jit(solution)/shard_map/all_to_all | solution.py:259
  33.4 2.8 %collective-permute-start.3 = (bf16[8,6,96,128]{3,2,1,0:T(8,128)(2,1)S(1)}, bf16[8,6,96,128]{3,2,1,0:T(8,128)(2,1)}, u32[]{:S(2)}, u32[]{:S(2)}) collective-permute-start(bf16[8,6,96,128]{3,2,1,0:T(8,128)(2,1)S(1)} %all-to-all-done.1), channel_id=1, source_target_pairs={{8,0},{16,8},{24,16},{32,24},{40,32},{48,40},{56,48},{64,56},{72,6... | collective-permute-start | bytes 3538952 | tf_op jit(solution)/shard_map/ppermute | solution.py:265
  36.2 3.4 %collective-permute-start.2 = (bf16[8,6,96,128]{3,2,1,0:T(8,128)(2,1)S(1)}, bf16[8,6,96,128]{3,2,1,0:T(8,128)(2,1)}, u32[]{:S(2)}, u32[]{:S(2)}) collective-permute-start(bf16[8,6,96,128]{3,2,1,0:T(8,128)(2,1)S(1)} %all-to-all-done.1), channel_id=1, source_target_pairs={{0,8},{8,16},{16,24},{24,32},{32,40},{40,48},{48,56},{56,64},{64,7... | collective-permute-start | bytes 3538952 | tf_op jit(solution)/shard_map/ppermute | solution.py:264
  39.6 0.0 copy-done
  39.6 0.6 slice_reduce_fusion
  40.9 17.5 %all-to-all-done = bf16[8,9,96,128]{3,2,1,0:T(8,128)(2,1)S(1)} async-done(((bf16[8,9,96,128]{3,2,1,0:T(8,128)(2,1)}), bf16[8,9,96,128]{3,2,1,0:T(8,128)(2,1)S(1)}, u32[]{:S(2)}, u32[]{:S(2)}) %all-to-all-start) | async-done | bytes 1769504 | tf_op jit(solution)/shard_map/all_to_all | solution.py:259
  58.4 0.0 collective-permute-done.3
  58.4 0.0 collective-permute-done.2
  58.4 11.3 %conditional.1 = (bf16[8,5,96,128]{3,2,1,0:T(8,128)(2,1)}) conditional(s32[]{:T(128)} %convert_element_type.3, (s32[40]{0:T(128)S(1)}, s32[3,40]{1,0:T(4,128)S(1)}, bf16[8,9,96,128]{3,2,1,0:T(8,128)(2,1)S(1)}, bf16[8,6,96,128]{3,2,1,0:T(8,128)(2,1)S(1)}, bf16[8,6,96,128]{3,2,1,0:T(8,128)(2,1)}, ...), branch_computations={%region_1.0_spmd, %region_2.0_spmd} | conditional | flops 3019898880 | bytes 15728728 | solution.py:305
  58.4 11.0 %attend_near_slots_wide.1 = bf16[8,5,96,128]{3,2,1,0:T(8,128)(2,1)} custom-call(s32[40]{0:T(128)S(1)} %get-tuple-element.32.order, s32[3,40]{1,0:T(4,128)S(1)} %get-tuple-element.33.windows, bf16[8,9,96,128]{3,2,1,0:T(8,128)(2,1)S(1)} %get-tuple-element.34.rest, bf16[8,6,96,128]{3,2,1,0:T(8,128)(2,1)S(1)} %get-tuple-element.35.near_kv, ...), custom_call_target="tpu_custom_call" | custom-call | flops 3019898880 | bytes 7864320 | tf_op jit(solution)/shard_map/cond/branch_0_fun/attend_near_slots_wide/pallas_call | solution.py:216
  69.7 21.2 %all_to_all.15.blocks = bf16[8,5,96,128]{3,2,1,0:T(8,128)(2,1)} all-to-all(bf16[8,5,96,128]{3,2,1,0:T(8,128)(2,1)} %get-tuple-element.48), channel_id=1, replica_groups=mesh['cfg'=2,'seq'=32,'head'=8] {'head'}, dimensions={0} | all-to-all | bytes 1966080 | tf_op jit(solution)/shard_map/all_to_all | solution.py:259
  90.8 2.1 %unpack_attended.1 = bf16[96,5120]{1,0:T(8,128)(2,1)} custom-call(s32[40]{0:T(128)S(1)} %get-tuple-element.46.order, bf16[8,5,96,128]{3,2,1,0:T(8,128)(2,1)} %all_to_all.15.blocks), custom_call_target="tpu_custom_call" | custom-call | bytes 1966080 | tf_op jit(solution)/shard_map/unpack_attended/pallas_call | solution.py:307
Async XLA Ops:
  3.6 26.2 %all-to-all-start.1 = ((bf16[8,6,96,128]{3,2,1,0:T(8,128)(2,1)}), bf16[8,6,96,128]{3,2,1,0:T(8,128)(2,1)S(1)}, u32[]{:S(2)}, u32[]{:S(2)}) async-start(bf16[8,6,96,128]{3,2,1,0:T(8,128)(2,1)} %get-tuple-element.47), calls=%async_computation.1 | async-start | bytes 2359296 | tf_op jit(solution)/shard_map/all_to_all | solution.py:259
  14.1 25.6 %copy-start = (s32[40,3]{0,1:T(4,128)S(1)}, s32[40,3]{0,1:T(4,128)}, u32[]{:S(2)}) copy-start(s32[40,3]{0,1:T(4,128)} %param.9) | copy-start | bytes 1444
  29.8 28.6 %all-to-all-start = ((bf16[8,9,96,128]{3,2,1,0:T(8,128)(2,1)}), bf16[8,9,96,128]{3,2,1,0:T(8,128)(2,1)S(1)}, u32[]{:S(2)}, u32[]{:S(2)}) async-start(bf16[8,9,96,128]{3,2,1,0:T(8,128)(2,1)} %pack_queries_and_rest.1), calls=%async_computation | async-start | bytes 3538944 | tf_op jit(solution)/shard_map/all_to_all | solution.py:259
  33.4 25.0 %collective-permute-start.3 = (bf16[8,6,96,128]{3,2,1,0:T(8,128)(2,1)S(1)}, bf16[8,6,96,128]{3,2,1,0:T(8,128)(2,1)}, u32[]{:S(2)}, u32[]{:S(2)}) collective-permute-start(bf16[8,6,96,128]{3,2,1,0:T(8,128)(2,1)S(1)} %all-to-all-done.1), channel_id=1, source_target_pairs={{8,0},{16,8},{24,16},{32,24},{40,32},{48,40},{56,48},{64,56},{72,6... | collective-permute-start | bytes 3538952 | tf_op jit(solution)/shard_map/ppermute | solution.py:265
  36.2 22.2 %collective-permute-start.2 = (bf16[8,6,96,128]{3,2,1,0:T(8,128)(2,1)S(1)}, bf16[8,6,96,128]{3,2,1,0:T(8,128)(2,1)}, u32[]{:S(2)}, u32[]{:S(2)}) collective-permute-start(bf16[8,6,96,128]{3,2,1,0:T(8,128)(2,1)S(1)} %all-to-all-done.1), channel_id=1, source_target_pairs={{0,8},{8,16},{16,24},{24,32},{32,40},{40,48},{48,56},{56,64},{64,7... | collective-permute-start | bytes 3538952 | tf_op jit(solution)/shard_map/ppermute | solution.py:264
